TPU v7x, 512 devices: a whole 4x8x8 slice. The times are simulated.
512 devices in a mesh: dp: 32 (over y_hi, x, core), ctx: 16 (over z, y_lo).
Axes of the slice: x: 4, y: 8 (y_hi: 4, y_lo: 2; y = y_hi * 2 + y_lo), z: 8, core: 2. Of those that a mesh axis runs over, the one named last changes fastest.
Arguments:
- hidden_in: bfloat16 [32, 2048, 4096], P('dp', 'ctx'), may hold values from -100 to 100
- query_states: bfloat16 [32, 2048, 256], P('dp', 'ctx'), may hold values from -80 to 80
- key_states: bfloat16 [32, 2048, 128], P('dp', 'ctx'), may hold values from -4 to 4
- value_states: bfloat16 [32, 2048, 128], P('dp', 'ctx'), may hold values from -6 to 6
- out_grad: bfloat16 [32, 2048, 256], P('dp', 'ctx'), may hold values from -6 to 6
- span_order: int32 [32, 32], P('dp'), may hold values from 0 to 31, each once within a row
Outputs:
- clipped_sum: float32 [4096, 512], P('ctx')
Inputs may be any that keep to these rules, and one draw needn't show every extreme that they name: Slot s of example e is the stored tokens s * 64 to (s + 1) * 64 - 1; each row of span_order is a permutation of the slots' sequence blocks.
All inputs are finite; a program needn't handle non-finite values.
Results may differ from a plain program's by a relative error of at most 0.0041.
Values may be sent and summed in bfloat16 or wider, within the bound.
A program may use at most 64 MiB of HBM per device.

v0:
```python
import math

import jax
import jax.numpy as jnp
from jax import lax
from jax.sharding import PartitionSpec as P

masked_fill = -1e30
gamma_floor = 0.01


def shifted(block, axis, distance):
    devices = range(lax.axis_size(axis))
    route = [((i - distance) % len(devices), i) for i in devices]
    return lax.ppermute(block, axis, route)


def slot_positions(span_table, first_row, row_count, span_len):
    global_rows = first_row + jnp.arange(row_count, dtype=jnp.int32)
    slot_ids = global_rows // span_len
    table_ids = jnp.arange(span_table.shape[0], dtype=jnp.int32)
    picked = jnp.sum(
        jnp.where(slot_ids[:, None] == table_ids[None, :], span_table[None, :], 0), axis=1
    )
    return picked * span_len + global_rows % span_len


def contract_last(left_rows, right_rows):
    return lax.dot_general(
        left_rows, right_rows, (((1,), (1,)), ((), ())), preferred_element_type=jnp.float32
    )


def contract_first(left_rows, right_rows):
    return lax.dot_general(
        left_rows, right_rows, (((0,), (0,)), ((), ())), preferred_element_type=jnp.float32
    )


def on_device(hidden_in, query_states, key_states, value_states, out_grad, span_order):
    cycle_size = lax.axis_size("ctx")
    my_index = lax.axis_index("ctx")
    tok_rows = query_states.shape[1]
    span_len = tok_rows // 2
    head_dim = key_states.shape[2]
    head_count = query_states.shape[2] // head_dim
    inv_scale = 1.0 / math.sqrt(head_dim)
    span_table = span_order[0]
    query_rows = query_states[0].reshape(tok_rows * head_count, head_dim)
    grad_rows = out_grad[0].reshape(tok_rows * head_count, head_dim)
    local_keys = key_states[0]
    local_values = value_states[0]
    own_pos = slot_positions(span_table, my_index * tok_rows, tok_rows, span_len)
    query_pos = jnp.repeat(own_pos, head_count)
    total_rows = tok_rows * head_count
    run_max = jnp.full((total_rows,), masked_fill, jnp.float32)
    key_block = lax.all_gather(local_keys, "ctx", axis=0, tiled=True)
    value_block = lax.all_gather(local_values, "ctx", axis=0, tiled=True)
    key_pos = slot_positions(span_table, jnp.int32(0), key_block.shape[0], span_len)
    allowed = key_pos[None, :] <= query_pos[:, None]
    scores = jnp.where(allowed, contract_last(query_rows, key_block) * inv_scale, masked_fill)
    grad_probs = contract_last(grad_rows, value_block)
    new_max = jnp.maximum(run_max, jnp.max(scores, axis=1))
    weights = jnp.exp(scores - new_max[:, None])
    run_sum = jnp.sum(weights, axis=1)
    run_dot = jnp.sum(weights * grad_probs, axis=1)
    log_total = new_max + jnp.log(run_sum)
    row_delta = run_dot / run_sum

    def tile_grads(key_block, value_block, key_pos):
        allowed = key_pos[None, :] <= query_pos[:, None]
        scores = jnp.where(allowed, contract_last(query_rows, key_block) * inv_scale, masked_fill)
        weights = jnp.where(allowed, jnp.exp(scores - log_total[:, None]), 0.0)
        grad_probs = contract_last(grad_rows, value_block)
        grad_scores = weights * (grad_probs - row_delta[:, None])
        scores_low = grad_scores.astype(jnp.bfloat16)
        weights_low = weights.astype(jnp.bfloat16)
        query_add = jnp.dot(scores_low, key_block, preferred_element_type=jnp.float32) * inv_scale
        key_add = contract_first(scores_low, query_rows) * inv_scale
        value_add = contract_first(weights_low, grad_rows)
        return (query_add, key_add, value_add)

    query_start = jnp.zeros((total_rows, head_dim), jnp.float32)

    def cycle_turn(turn_idx, carried):
        query_acc, key_block, value_block, key_acc, value_acc = carried
        source = (my_index - turn_idx) % cycle_size
        key_pos = slot_positions(span_table, source * tok_rows, tok_rows, span_len)
        query_add, key_add, value_add = tile_grads(key_block, value_block, key_pos)
        key_block, value_block = shifted((key_block, value_block), "ctx", 1)
        key_acc, value_acc = shifted((key_acc + key_add, value_acc + value_add), "ctx", 1)
        return (query_acc + query_add, key_block, value_block, key_acc, value_acc)

    acc_start = jnp.zeros((tok_rows, head_dim), jnp.float32)
    query_acc, unused_keys, unused_values, key_acc, value_acc = lax.fori_loop(
        0, cycle_size, cycle_turn, (query_start, local_keys, local_values, acc_start, acc_start)
    )
    query_grad = query_acc.reshape(tok_rows, head_count * head_dim).astype(jnp.bfloat16)
    local_grads = jnp.concatenate(
        [query_grad, key_acc.astype(jnp.bfloat16), value_acc.astype(jnp.bfloat16)], axis=1
    )
    feature_cols = lax.all_to_all(hidden_in[0], "ctx", split_axis=1, concat_axis=0, tiled=True)
    block_grad = contract_first(
        feature_cols, lax.all_gather(local_grads, "ctx", axis=0, tiled=True)
    )
    total_sq = lax.psum(jnp.sum(block_grad * block_grad), "ctx")
    model_width = hidden_in.shape[2]
    factor = math.sqrt(model_width * local_grads.shape[1] / lax.axis_size("dp")) / (
        jnp.sqrt(total_sq) + gamma_floor
    )
    return lax.psum(block_grad * factor, "dp")


def solution(mesh):
    return jax.shard_map(
        on_device,
        mesh=mesh,
        in_specs=(
            P("dp", "ctx", None),
            P("dp", "ctx", None),
            P("dp", "ctx", None),
            P("dp", "ctx", None),
            P("dp", "ctx", None),
            P("dp", None),
        ),
        out_specs=P("ctx", None),
        check_vma=False,
    )
```

profile of v0, /device:TPU:1, one launch (start us, length us, event | category | flops | bytes accessed | tf_op | source)
XLA Modules:
  0.0 789.1 jit_solution(5638749991920912825)
XLA Ops:
  9.1 38.4 %all-gather = bf16[1,2048,128]{2,1,0:T(8,128)(2,1)S(1)} all-gather(bf16[1,128,128]{2,1,0:T(8,128)(2,1)S(1)} %copy.36), channel_id=2, replica_groups=mesh['dp'=32,'ctx'=16] {'ctx'}, dimensions={1}, use_global_device_ids=true | all-gather | bytes 557056 | tf_op jit(solution)/shard_map/all_gather | solution.py:57
  49.7 27.8 %all-gather.1 = bf16[1,2048,128]{2,1,0:T(8,128)(2,1)S(1)} all-gather(bf16[1,128,128]{2,1,0:T(8,128)(2,1)S(1)} %copy.37), channel_id=3, replica_groups=mesh['dp'=32,'ctx'=16] {'ctx'}, dimensions={1}, use_global_device_ids=true | all-gather | bytes 557056 | tf_op jit(solution)/shard_map/all_gather | solution.py:58
  78.5 254.3 %while.25 = (s32[]{:T(128)}, f32[256,128]{1,0:T(8,128)S(1)}, bf16[128,128]{1,0:T(8,128)(2,1)S(1)}, bf16[128,128]{1,0:T(8,128)(2,1)S(1)}, f32[128,128]{1,0:T(8,12...) while((s32[]{:T(128)}, f32[256,128]{1,0:T(8,128)S(1)}, ...), condition=%wide.region_7.8_spmd.clone, body=%wide.region_5.7_spmd.clone.sunk | while | flops 42401424 | bytes 2402396 | solution.py:95
  109.5 3.4 collective-permute-start.1
  116.5 3.4 collective-permute-start.3
  125.5 3.8 collective-permute-start.1
  132.4 3.8 collective-permute-start.3
  142.1 3.7 collective-permute-start.1
  149.6 4.3 collective-permute-start.3
  159.5 4.7 collective-permute-start.1
  227.8 4.9 collective-permute-start.3
  237.7 4.6 collective-permute-start.1
  250.4 3.6 collective-permute-done.3
  255.9 3.6 collective-permute-start.1
  291.0 3.9 collective-permute-start.3
  300.5 3.8 collective-permute-start.1
  307.4 3.4 collective-permute-start.3
  316.6 3.9 collective-permute-start.1
  321.5 4.1 collective-permute-start.2
  325.7 3.9 collective-permute-start.3
  334.4 20.1 %all_to_all.19 = bf16[128,16,256]{0,2,1:T(8,128)(2,1)S(1)} all-to-all(bf16[128,16,256]{0,2,1:T(8,128)(2,1)S(1)} %bitcast.51), channel_id=1, replica_groups=mesh['dp'=32,'ctx'=16] {'ctx'}, dimensions={1} | all-to-all | bytes 2097152 | tf_op jit(solution)/shard_map/all_to_all | solution.py:102
  355.0 89.5 %all-gather.4.cloned.1.call-done = bf16[2048,512]{1,0:T(8,128)(2,1)} async-done(((bf16[128,512]{1,0:T(8,128)(2,1)}), bf16[2048,512]{1,0:T(8,128)(2,1)}) %all-gather.4.cloned.1.call-update) | async-done | bytes 2097168 | tf_op jit(solution)/shard_map/all_gather | solution.py:104
  447.4 26.9 %psum.14 = f32[]{:T(128)} all-reduce(f32[]{:T(128)} %get-tuple-element.437), channel_id=1, replica_groups=mesh['dp'=32,'ctx'=16] {'ctx'}, use_global_device_ids=true, to_apply=%region_9.10 | all-reduce | flops 1 | bytes 8 | tf_op jit(solution)/shard_map/psum | solution.py:106
  475.9 304.3 %all-reduce.2.cloned.1.call-done = f32[256,512]{0,1:T(8,128)} async-done(((f32[256,512]{0,1:T(8,128)}), f32[256,512]{0,1:T(8,128)}) %all-reduce.2.cloned.1.call-update) | async-done | bytes 524304 | tf_op jit(solution)/shard_map/psum | solution.py:111
  (343 shorter events, 199.0 us)
Async XLA Ops:
  6.5 438.0 %all-gather.4.cloned.1.call-start = ((), (), s32[]{:S(2)}) async-start(), calls=%async_computation.1 | async-start | bytes 2228224 | tf_op jit(solution)/shard_map/all_gather | solution.py:104
  93.1 10.4 %collective-permute-start = (bf16[128,128]{1,0:T(8,128)(2,1)S(1)}, bf16[128,128]{1,0:T(8,128)(2,1)S(1)}, u32[]{:S(2)}, u32[]{:S(2)}) collective-permute-start(bf16[128,128]{1,0:T(8,128)(2,1)S(1)} %copy.23), channel_id=1, source_target_pairs={{15,0},{0,1},{1,2},{2,3},{3,4},{4,5},{5,6},{6,7},{7,8},{8,9},{9,10... | collective-permute-start | bytes 98312 | tf_op jit(solution)/shard_map/while/body/eval_jaxpr/ppermute | solution.py:15
  107.6 12.5 %collective-permute-start = (bf16[128,128]{1,0:T(8,128)(2,1)S(1)}, bf16[128,128]{1,0:T(8,128)(2,1)S(1)}, u32[]{:S(2)}, u32[]{:S(2)}) collective-permute-start(bf16[128,128]{1,0:T(8,128)(2,1)S(1)} %copy.23), channel_id=1, source_target_pairs={{15,0},{0,1},{1,2},{2,3},{3,4},{4,5},{5,6},{6,7},{7,8},{8,9},{9,10... | collective-permute-start | bytes 98312 | tf_op jit(solution)/shard_map/while/body/eval_jaxpr/ppermute | solution.py:15
  109.5 10.6 %collective-permute-start.1 = (bf16[128,128]{1,0:T(8,128)(2,1)S(1)}, bf16[128,128]{1,0:T(8,128)(2,1)S(1)}, u32[]{:S(2)}, u32[]{:S(2)}) collective-permute-start(bf16[128,128]{1,0:T(8,128)(2,1)S(1)} %copy.24), channel_id=1, source_target_pairs={{15,0},{0,1},{1,2},{2,3},{3,4},{4,5},{5,6},{6,7},{7,8},{8,9},{9,10... | collective-permute-start | bytes 98312 | tf_op jit(solution)/shard_map/while/body/eval_jaxpr/ppermute | solution.py:15
  123.6 12.8 %collective-permute-start = (bf16[128,128]{1,0:T(8,128)(2,1)S(1)}, bf16[128,128]{1,0:T(8,128)(2,1)S(1)}, u32[]{:S(2)}, u32[]{:S(2)}) collective-permute-start(bf16[128,128]{1,0:T(8,128)(2,1)S(1)} %copy.23), channel_id=1, source_target_pairs={{15,0},{0,1},{1,2},{2,3},{3,4},{4,5},{5,6},{6,7},{7,8},{8,9},{9,10... | collective-permute-start | bytes 98312 | tf_op jit(solution)/shard_map/while/body/eval_jaxpr/ppermute | solution.py:15
  125.5 10.8 %collective-permute-start.1 = (bf16[128,128]{1,0:T(8,128)(2,1)S(1)}, bf16[128,128]{1,0:T(8,128)(2,1)S(1)}, u32[]{:S(2)}, u32[]{:S(2)}) collective-permute-start(bf16[128,128]{1,0:T(8,128)(2,1)S(1)} %copy.24), channel_id=1, source_target_pairs={{15,0},{0,1},{1,2},{2,3},{3,4},{4,5},{5,6},{6,7},{7,8},{8,9},{9,10... | collective-permute-start | bytes 98312 | tf_op jit(solution)/shard_map/while/body/eval_jaxpr/ppermute | solution.py:15
  139.5 14.5 %collective-permute-start = (bf16[128,128]{1,0:T(8,128)(2,1)S(1)}, bf16[128,128]{1,0:T(8,128)(2,1)S(1)}, u32[]{:S(2)}, u32[]{:S(2)}) collective-permute-start(bf16[128,128]{1,0:T(8,128)(2,1)S(1)} %copy.23), channel_id=1, source_target_pairs={{15,0},{0,1},{1,2},{2,3},{3,4},{4,5},{5,6},{6,7},{7,8},{8,9},{9,10... | collective-permute-start | bytes 98312 | tf_op jit(solution)/shard_map/while/body/eval_jaxpr/ppermute | solution.py:15
  142.1 12.0 %collective-permute-start.1 = (bf16[128,128]{1,0:T(8,128)(2,1)S(1)}, bf16[128,128]{1,0:T(8,128)(2,1)S(1)}, u32[]{:S(2)}, u32[]{:S(2)}) collective-permute-start(bf16[128,128]{1,0:T(8,128)(2,1)S(1)} %copy.24), channel_id=1, source_target_pairs={{15,0},{0,1},{1,2},{2,3},{3,4},{4,5},{5,6},{6,7},{7,8},{8,9},{9,10... | collective-permute-start | bytes 98312 | tf_op jit(solution)/shard_map/while/body/eval_jaxpr/ppermute | solution.py:15
  156.7 13.3 %collective-permute-start = (bf16[128,128]{1,0:T(8,128)(2,1)S(1)}, bf16[128,128]{1,0:T(8,128)(2,1)S(1)}, u32[]{:S(2)}, u32[]{:S(2)}) collective-permute-start(bf16[128,128]{1,0:T(8,128)(2,1)S(1)} %copy.23), channel_id=1, source_target_pairs={{15,0},{0,1},{1,2},{2,3},{3,4},{4,5},{5,6},{6,7},{7,8},{8,9},{9,10... | collective-permute-start | bytes 98312 | tf_op jit(solution)/shard_map/while/body/eval_jaxpr/ppermute | solution.py:15
  159.5 10.5 %collective-permute-start.1 = (bf16[128,128]{1,0:T(8,128)(2,1)S(1)}, bf16[128,128]{1,0:T(8,128)(2,1)S(1)}, u32[]{:S(2)}, u32[]{:S(2)}) collective-permute-start(bf16[128,128]{1,0:T(8,128)(2,1)S(1)} %copy.24), channel_id=1, source_target_pairs={{15,0},{0,1},{1,2},{2,3},{3,4},{4,5},{5,6},{6,7},{7,8},{8,9},{9,10... | collective-permute-start | bytes 98312 | tf_op jit(solution)/shard_map/while/body/eval_jaxpr/ppermute | solution.py:15
  189.1 9.8 %collective-permute-start = (bf16[128,128]{1,0:T(8,128)(2,1)S(1)}, bf16[128,128]{1,0:T(8,128)(2,1)S(1)}, u32[]{:S(2)}, u32[]{:S(2)}) collective-permute-start(bf16[128,128]{1,0:T(8,128)(2,1)S(1)} %copy.23), channel_id=1, source_target_pairs={{15,0},{0,1},{1,2},{2,3},{3,4},{4,5},{5,6},{6,7},{7,8},{8,9},{9,10... | collective-permute-start | bytes 98312 | tf_op jit(solution)/shard_map/while/body/eval_jaxpr/ppermute | solution.py:15
  203.2 11.6 %collective-permute-start = (bf16[128,128]{1,0:T(8,128)(2,1)S(1)}, bf16[128,128]{1,0:T(8,128)(2,1)S(1)}, u32[]{:S(2)}, u32[]{:S(2)}) collective-permute-start(bf16[128,128]{1,0:T(8,128)(2,1)S(1)} %copy.23), channel_id=1, source_target_pairs={{15,0},{0,1},{1,2},{2,3},{3,4},{4,5},{5,6},{6,7},{7,8},{8,9},{9,10... | collective-permute-start | bytes 98312 | tf_op jit(solution)/shard_map/while/body/eval_jaxpr/ppermute | solution.py:15
  205.1 9.7 %collective-permute-start.1 = (bf16[128,128]{1,0:T(8,128)(2,1)S(1)}, bf16[128,128]{1,0:T(8,128)(2,1)S(1)}, u32[]{:S(2)}, u32[]{:S(2)}) collective-permute-start(bf16[128,128]{1,0:T(8,128)(2,1)S(1)} %copy.24), channel_id=1, source_target_pairs={{15,0},{0,1},{1,2},{2,3},{3,4},{4,5},{5,6},{6,7},{7,8},{8,9},{9,10... | collective-permute-start | bytes 98312 | tf_op jit(solution)/shard_map/while/body/eval_jaxpr/ppermute | solution.py:15
  218.9 14.0 %collective-permute-start = (bf16[128,128]{1,0:T(8,128)(2,1)S(1)}, bf16[128,128]{1,0:T(8,128)(2,1)S(1)}, u32[]{:S(2)}, u32[]{:S(2)}) collective-permute-start(bf16[128,128]{1,0:T(8,128)(2,1)S(1)} %copy.23), channel_id=1, source_target_pairs={{15,0},{0,1},{1,2},{2,3},{3,4},{4,5},{5,6},{6,7},{7,8},{8,9},{9,10... | collective-permute-start | bytes 98312 | tf_op jit(solution)/shard_map/while/body/eval_jaxpr/ppermute | solution.py:15
  220.9 12.1 %collective-permute-start.1 = (bf16[128,128]{1,0:T(8,128)(2,1)S(1)}, bf16[128,128]{1,0:T(8,128)(2,1)S(1)}, u32[]{:S(2)}, u32[]{:S(2)}) collective-permute-start(bf16[128,128]{1,0:T(8,128)(2,1)S(1)} %copy.24), channel_id=1, source_target_pairs={{15,0},{0,1},{1,2},{2,3},{3,4},{4,5},{5,6},{6,7},{7,8},{8,9},{9,10... | collective-permute-start | bytes 98312 | tf_op jit(solution)/shard_map/while/body/eval_jaxpr/ppermute | solution.py:15
  234.9 15.0 %collective-permute-start = (bf16[128,128]{1,0:T(8,128)(2,1)S(1)}, bf16[128,128]{1,0:T(8,128)(2,1)S(1)}, u32[]{:S(2)}, u32[]{:S(2)}) collective-permute-start(bf16[128,128]{1,0:T(8,128)(2,1)S(1)} %copy.23), channel_id=1, source_target_pairs={{15,0},{0,1},{1,2},{2,3},{3,4},{4,5},{5,6},{6,7},{7,8},{8,9},{9,10... | collective-permute-start | bytes 98312 | tf_op jit(solution)/shard_map/while/body/eval_jaxpr/ppermute | solution.py:15
  237.7 12.2 %collective-permute-start.1 = (bf16[128,128]{1,0:T(8,128)(2,1)S(1)}, bf16[128,128]{1,0:T(8,128)(2,1)S(1)}, u32[]{:S(2)}, u32[]{:S(2)}) collective-permute-start(bf16[128,128]{1,0:T(8,128)(2,1)S(1)} %copy.24), channel_id=1, source_target_pairs={{15,0},{0,1},{1,2},{2,3},{3,4},{4,5},{5,6},{6,7},{7,8},{8,9},{9,10... | collective-permute-start | bytes 98312 | tf_op jit(solution)/shard_map/while/body/eval_jaxpr/ppermute | solution.py:15
  254.0 11.2 %collective-permute-start = (bf16[128,128]{1,0:T(8,128)(2,1)S(1)}, bf16[128,128]{1,0:T(8,128)(2,1)S(1)}, u32[]{:S(2)}, u32[]{:S(2)}) collective-permute-start(bf16[128,128]{1,0:T(8,128)(2,1)S(1)} %copy.23), channel_id=1, source_target_pairs={{15,0},{0,1},{1,2},{2,3},{3,4},{4,5},{5,6},{6,7},{7,8},{8,9},{9,10... | collective-permute-start | bytes 98312 | tf_op jit(solution)/shard_map/while/body/eval_jaxpr/ppermute | solution.py:15
  284.1 11.1 %collective-permute-start = (bf16[128,128]{1,0:T(8,128)(2,1)S(1)}, bf16[128,128]{1,0:T(8,128)(2,1)S(1)}, u32[]{:S(2)}, u32[]{:S(2)}) collective-permute-start(bf16[128,128]{1,0:T(8,128)(2,1)S(1)} %copy.23), channel_id=1, source_target_pairs={{15,0},{0,1},{1,2},{2,3},{3,4},{4,5},{5,6},{6,7},{7,8},{8,9},{9,10... | collective-permute-start | bytes 98312 | tf_op jit(solution)/shard_map/while/body/eval_jaxpr/ppermute | solution.py:15
  298.6 12.4 %collective-permute-start = (bf16[128,128]{1,0:T(8,128)(2,1)S(1)}, bf16[128,128]{1,0:T(8,128)(2,1)S(1)}, u32[]{:S(2)}, u32[]{:S(2)}) collective-permute-start(bf16[128,128]{1,0:T(8,128)(2,1)S(1)} %copy.23), channel_id=1, source_target_pairs={{15,0},{0,1},{1,2},{2,3},{3,4},{4,5},{5,6},{6,7},{7,8},{8,9},{9,10... | collective-permute-start | bytes 98312 | tf_op jit(solution)/shard_map/while/body/eval_jaxpr/ppermute | solution.py:15
  300.5 10.5 %collective-permute-start.1 = (bf16[128,128]{1,0:T(8,128)(2,1)S(1)}, bf16[128,128]{1,0:T(8,128)(2,1)S(1)}, u32[]{:S(2)}, u32[]{:S(2)}) collective-permute-start(bf16[128,128]{1,0:T(8,128)(2,1)S(1)} %copy.24), channel_id=1, source_target_pairs={{15,0},{0,1},{1,2},{2,3},{3,4},{4,5},{5,6},{6,7},{7,8},{8,9},{9,10... | collective-permute-start | bytes 98312 | tf_op jit(solution)/shard_map/while/body/eval_jaxpr/ppermute | solution.py:15
  314.7 15.2 %collective-permute-start = (bf16[128,128]{1,0:T(8,128)(2,1)S(1)}, bf16[128,128]{1,0:T(8,128)(2,1)S(1)}, u32[]{:S(2)}, u32[]{:S(2)}) collective-permute-start(bf16[128,128]{1,0:T(8,128)(2,1)S(1)} %copy.23), channel_id=1, source_target_pairs={{15,0},{0,1},{1,2},{2,3},{3,4},{4,5},{5,6},{6,7},{7,8},{8,9},{9,10... | collective-permute-start | bytes 98312 | tf_op jit(solution)/shard_map/while/body/eval_jaxpr/ppermute | solution.py:15
  316.6 13.3 %collective-permute-start.1 = (bf16[128,128]{1,0:T(8,128)(2,1)S(1)}, bf16[128,128]{1,0:T(8,128)(2,1)S(1)}, u32[]{:S(2)}, u32[]{:S(2)}) collective-permute-start(bf16[128,128]{1,0:T(8,128)(2,1)S(1)} %copy.24), channel_id=1, source_target_pairs={{15,0},{0,1},{1,2},{2,3},{3,4},{4,5},{5,6},{6,7},{7,8},{8,9},{9,10... | collective-permute-start | bytes 98312 | tf_op jit(solution)/shard_map/while/body/eval_jaxpr/ppermute | solution.py:15
  333.6 446.6 %all-reduce.2.cloned.1.call-start = ((), (), s32[]{:S(2)}) async-start(), calls=%async_computation.2 | async-start | bytes 1048576 | tf_op jit(solution)/shard_map/psum | solution.py:111
  (45 other events, 641.5 us)
Sparse Core Ops, SparseCore 0:
  333.7 110.7 all-gather.3
  476.0 304.1 all-reduce.1
where the time goes:
time: 791 us; the launch traced here: 789 us
  waiting for transfers between devices  456 us (58%)
  starting transfers between devices  170 us (21%)
  blocking collectives  113 us (14%)
  matrix products  18.8 us (2%)
  between operations  14.3 us (2%)
  local copies, waits for them, and re-layouts  9.57 us (1%)
    psum x1, waiting for transfers between devices, on_device(): return lax.psum(block_grad * factor, 'dp')  304 us
    ppermute x64, starting transfers between devices, shifted(): return lax.ppermute(block, axis, route)  170 us
    all_gather x1, waiting for transfers between devices, on_device(): lax.all_gather(local_grads, 'ctx', axis=0, tiled=True)  89.5 us
    ppermute x64, waiting for transfers between devices, shifted(): return lax.ppermute(block, axis, route)  62 us
    all_gather x1, blocking collectives, on_device(): key_block = lax.all_gather(local_keys, 'ctx', axis=0, tiled=True)  38.4 us
    all_gather x1, blocking collectives, on_device(): value_block = lax.all_gather(local_values, 'ctx', axis=0, tiled=True)  27.8 us
    psum x1, blocking collectives, on_device(): total_sq = lax.psum(jnp.sum(block_grad * block_grad), 'ctx')  26.9 us
    all_to_all x1, blocking collectives, on_device(): lax.all_to_all(hidden_in[0], 'ctx', split_axis=1, concat_axis=0, tiled=True)  20.1 us
  transfers between devices with their start and end apart: 66, of which 32 were waited for; matrix products, arithmetic and copies ran while one was open for 3% of the time, Pallas kernels for 0%

commit v1 on v0

v1 whole, which is shorter than its diff:
```python
import functools
import math

import jax
import jax.numpy as jnp
from jax import lax
from jax.experimental import pallas as pl
from jax.experimental.pallas import tpu as pltpu
from jax.sharding import PartitionSpec as P

MESH = pl.DeviceIdType.MESH
F32 = jnp.float32
BF16 = jnp.bfloat16

masked_fill = -1e30
gamma_floor = 0.01

TOK = 128
HEAD = 128
SPAN = 64
NZ = 8
FEAT = 256
COLS = 512
CHIPS = 16


def aligned(index, size):
    return pl.ds(pl.multiple_of(index * size, size), size)


def contract(left, right, left_dim, right_dim):
    return lax.dot_general(
        left, right, (((left_dim,), (right_dim,)), ((), ())), preferred_element_type=F32
    )


def kernel(
    scale_total,
    h_ref,
    q_ref,
    k_ref,
    v_ref,
    do_ref,
    span_ref,
    out_ref,
    hid,
    kv,
    qd,
    qs,
    stat_out,
    stat_in,
    expo,
    dprob,
    low_s,
    part_out,
    part_in,
    dq_out,
    dq_in,
    grads,
    acc,
    norm_box,
    half_in,
    fac_out,
    fac_in,
    rs_out,
    rs_in,
    ag,
    ag_far,
    hid_ss,
    hid_rs,
    ring_ss,
    ring_rs,
    pair_ss,
    pair_rs,
    fwd_ss,
    fwd_rs,
    part_ss,
    part_rs,
    norm_ss,
    norm_rs,
    rs_ss,
    rs_rs,
    ag_ss,
    ag_rs,
    own_sem,
):
    dp = lax.axis_index("dp")
    ctx = lax.axis_index("ctx")
    z = ctx // 2
    yl = lax.rem(ctx, 2)
    core = lax.rem(dp, 2)
    chip = dp // 2
    inv_scale = 1.0 / math.sqrt(HEAD)

    def zed(step):
        return lax.rem(z + step + NZ, NZ)

    up = (dp, zed(1) * 2 + yl)
    down = (dp, zed(-1) * 2 + yl)
    pair = (dp, z * 2 + (1 - yl))
    twin = (chip * 2 + (1 - core), ctx)

    def send(src, dst, ss, rs, device):
        copy = pltpu.make_async_remote_copy(
            src_ref=src, dst_ref=dst, send_sem=ss, recv_sem=rs,
            device_id=device, device_id_type=MESH,
        )
        copy.start()
        return copy

    barrier = pltpu.get_barrier_semaphore()
    for step in range(1, 16):
        pl.semaphore_signal(
            barrier, inc=1, device_id=(dp, lax.rem(ctx + step, 16)), device_id_type=MESH
        )
    for step in range(1, CHIPS):
        other = lax.rem(chip + step, CHIPS) * 2 + core
        pl.semaphore_signal(barrier, inc=1, device_id=(other, ctx), device_id_type=MESH)
    pl.semaphore_signal(barrier, inc=1, device_id=twin, device_id_type=MESH)

    kv[z, :, :HEAD] = k_ref[0]
    kv[z, :, HEAD:] = v_ref[0]
    qd[yl, :, : 2 * HEAD] = q_ref[0]
    qd[yl, :, 2 * HEAD :] = do_ref[0]
    pl.semaphore_wait(barrier, 31)

    started = []

    qd_copy = send(qd.at[yl], qd.at[yl], pair_ss.at[0], pair_rs.at[0], pair)

    def ring_send(lane, step, view_up, view_down):
        first = send(view_up, view_up, ring_ss.at[lane, 0, step], ring_rs.at[lane, 0, step], up)
        second = send(
            view_down, view_down, ring_ss.at[lane, 1, step], ring_rs.at[lane, 1, step], down
        )
        started.extend([first, second])
        return first, second

    def kv_views(step):
        if step < 4:
            return kv.at[zed(1 - step)], kv.at[zed(step - 1)]
        return kv.at[zed(-3), :, :HEAD], kv.at[zed(3), :, HEAD:]

    kv_copies = ring_send(0, 1, *kv_views(1))

    own_copy = pltpu.make_async_copy(
        h_ref.at[0, :, aligned(ctx, FEAT)], hid.at[z, aligned(yl, TOK), :], own_sem
    )
    own_copy.start()

    lane = lax.broadcasted_iota(jnp.int32, (1, 4 * HEAD), 1)
    token = lax.rem(lane, 2 * TOK)
    slot = token // SPAN
    first_slot = z * 4
    query_pos = jnp.full((1, 4 * HEAD), 0, jnp.int32)
    for s in range(4):
        query_pos = jnp.where(slot == s, span_ref[0, first_slot + s], query_pos)
    query_pos = query_pos * SPAN + lax.rem(token, SPAN)
    row = lax.broadcasted_iota(jnp.int32, (TOK, 4 * HEAD), 0)
    row_low = row < SPAN

    qd_copy.wait()
    for h in range(2):
        for y in range(2):
            rows = pl.ds(h * 2 * TOK + y * TOK, TOK)
            qs[0, rows, :] = qd[y, :, h * HEAD : (h + 1) * HEAD]
            qs[1, rows, :] = qd[y, :, (2 + h) * HEAD : (3 + h) * HEAD]

    tops, sums, dots = [], [], []

    def first_pass(place, block_z):
        keys = kv[block_z, :, :HEAD]
        values = kv[block_z, :, HEAD:]
        key_slot = (block_z * 2 + yl) * 2
        low = span_ref[0, key_slot] * SPAN
        high = span_ref[0, key_slot + 1] * SPAN - SPAN
        key_pos = jnp.where(row_low, low, high) + row
        raw = contract(keys, qs[0], 1, 1) * inv_scale
        scores = jnp.where(key_pos <= query_pos, raw, masked_fill)
        probs = contract(values, qs[1], 1, 1)
        top = jnp.max(scores, axis=0, keepdims=True)
        weights = jnp.exp(scores - top)
        expo[place] = weights
        dprob[place] = probs
        tops.append(top)
        sums.append(jnp.sum(weights, axis=0, keepdims=True))
        dots.append(jnp.sum(weights * probs, axis=0, keepdims=True))

    order = [0]
    first_pass(0, z)
    for step in range(1, 5):
        for copy in kv_copies:
            copy.wait_recv()
        if step < 4:
            kv_copies = ring_send(0, step + 1, *kv_views(step + 1))
            order += [-step, step]
            first_pass(2 * step - 1, zed(-step))
            first_pass(2 * step, zed(step))
        else:
            order += [4]
            first_pass(7, zed(4))

    hid_copies = []
    for step in [8, 9, 7, 10, 6, 11, 5, 12, 4, 13, 3, 14, 2, 15, 1]:
        peer = lax.rem(ctx + step, 16)
        hid_copies.append(
            send(
                h_ref.at[0, :, aligned(peer, FEAT)],
                hid.at[z, aligned(yl, TOK), :],
                hid_ss.at[step], hid_rs.at[step], (dp, peer),
            )
        )

    started.extend(hid_copies)

    top = functools.reduce(jnp.maximum, tops)
    total = sum(jnp.exp(t - top) * s for t, s in zip(tops, sums))
    dot = sum(jnp.exp(t - top) * d for t, d in zip(tops, dots))
    stat_out[...] = jnp.concatenate([top, total, dot] + [top] * 5, axis=0)
    send(stat_out, stat_in, pair_ss.at[1], pair_rs.at[1], pair).wait()
    far_top = stat_in[0:1, :]
    whole_top = jnp.maximum(top, far_top)
    mine, far = jnp.exp(top - whole_top), jnp.exp(far_top - whole_top)
    whole_sum = mine * total + far * stat_in[1:2, :]
    log_total = whole_top + jnp.log(whole_sum)
    row_delta = (mine * dot + far * stat_in[2:3, :]) / whole_sum

    part_copies = []
    own_part = None
    for place in [7, 5, 6, 3, 4, 1, 2, 0]:
        shift = order[place]
        probs = expo[place] * jnp.exp(tops[place] - log_total)
        scores_low = (probs * (dprob[place] - row_delta)).astype(BF16)
        low_s[place] = scores_low
        key_add = jnp.dot(scores_low, qs[0], preferred_element_type=F32) * inv_scale
        value_add = jnp.dot(probs.astype(BF16), qs[1], preferred_element_type=F32)
        if shift == 0:
            own_part = (key_add, value_add)
            continue
        part_out[place, :, :HEAD] = key_add.astype(BF16)
        part_out[place, :, HEAD:] = value_add.astype(BF16)
        part_copies.append(
            send(
                part_out.at[place], part_in.at[place],
                part_ss.at[place], part_rs.at[place], (dp, zed(shift) * 2 + yl),
            )
        )

    query_sum = jnp.zeros((HEAD, 4 * HEAD), F32)
    for place in range(8):
        query_sum += contract(kv[zed(order[place]), :, :HEAD], low_s[place], 0, 0)
    query_sum = query_sum.T * inv_scale
    acc[:, :HEAD] = query_sum[: 2 * TOK]
    acc[:, HEAD : 2 * HEAD] = query_sum[2 * TOK :]
    dq_out[...] = acc[aligned(1 - yl, TOK), : 2 * HEAD].astype(BF16)
    send(dq_out, dq_in, pair_ss.at[2], pair_rs.at[2], pair).wait()
    query_grad = acc[aligned(yl, TOK), : 2 * HEAD] + dq_in[...].astype(F32)
    grads[z, aligned(yl, TOK), : 2 * HEAD] = query_grad.astype(BF16)

    mine_rows = aligned(yl, TOK)

    def forward(lane, place, block_z, columns):
        view = grads.at[block_z, mine_rows, columns]
        copy = send(view, view, fwd_ss.at[lane, place], fwd_rs.at[lane, place], pair)
        started.append(copy)
        return copy

    def z_first(lane, start, width):
        half = width // 2

        def views(step):
            if step < 4:
                return (
                    grads.at[zed(1 - step), mine_rows, pl.ds(start, width)],
                    grads.at[zed(step - 1), mine_rows, pl.ds(start, width)],
                )
            if half >= 128:
                return (
                    grads.at[zed(-3), mine_rows, pl.ds(start, half)],
                    grads.at[zed(3), mine_rows, pl.ds(start + half, half)],
                )
            low = pl.ds(pl.multiple_of(yl * TOK, 64), TOK // 2)
            high = pl.ds(pl.multiple_of(yl * TOK + TOK // 2, 64), TOK // 2)
            return (
                grads.at[zed(-3), low, pl.ds(start, width)],
                grads.at[zed(3), high, pl.ds(start, width)],
            )

        columns = pl.ds(start, width)
        arrivals = [forward(lane, 0, z, columns)]
        copies = ring_send(lane, 1, *views(1))
        for step in range(1, 5):
            for copy in copies:
                copy.wait_recv()
            if step < 4:
                copies = ring_send(lane, step + 1, *views(step + 1))
                arrivals.append(forward(lane, 2 * step - 1, zed(-step), columns))
                arrivals.append(forward(lane, 2 * step, zed(step), columns))
            else:
                arrivals.append(forward(lane, 7, zed(4), columns))
            yield None
        yield arrivals

    def y_first(lane, start, width):
        columns = pl.ds(start, width)
        exchange = forward(lane, 0, z, columns)

        def views(step):
            if step < 4:
                return (
                    grads.at[zed(1 - step), :, columns],
                    grads.at[zed(step - 1), :, columns],
                )
            return (
                grads.at[zed(-3), pl.ds(0, TOK), columns],
                grads.at[zed(3), pl.ds(TOK, TOK), columns],
            )

        exchange.wait_recv()
        copies = ring_send(lane, 1, *views(1))
        for step in range(1, 5):
            for copy in copies:
                copy.wait_recv()
            if step < 4:
                copies = ring_send(lane, step + 1, *views(step + 1))
            yield None
        yield []

    query_arrivals = list(z_first(1, 0, 2 * HEAD))[-1]

    key_sum, value_sum = own_part
    for copy in part_copies:
        copy.wait_recv()
    for place in range(1, 8):
        key_sum = key_sum + part_in[place, :, :HEAD].astype(F32)
        value_sum = value_sum + part_in[place, :, HEAD:].astype(F32)
    grads[z, mine_rows, pl.ds(2 * HEAD, HEAD)] = key_sum.astype(BF16)
    grads[z, mine_rows, pl.ds(3 * HEAD, HEAD)] = value_sum.astype(BF16)

    value_lane = z_first(2, 3 * HEAD, HEAD)
    key_lane = y_first(3, 2 * HEAD, HEAD)
    arrivals = []
    for _ in range(5):
        arrivals = next(value_lane)
        next(key_lane)
    for copy in query_arrivals + arrivals:
        copy.wait_recv()
    own_copy.wait()
    for copy in hid_copies:
        copy.wait_recv()

    for block in range(NZ):
        part = contract(hid[block], grads[block], 0, 0)
        if block == 0:
            acc[...] = part
        else:
            acc[...] += part

    near_rows = aligned(core, TOK)
    half_copy = send(
        acc.at[aligned(1 - core, TOK)], half_in, pair_ss.at[3], pair_rs.at[3], twin
    )
    whole = acc[...]
    squares = jnp.sum((whole * whole).reshape(32, 8, COLS), axis=0)
    tile = squares[:, :128] + squares[:, 128:256] + squares[:, 256:384] + squares[:, 384:]
    norm_box[ctx] = tile
    norm_copies = []
    for step in range(1, 16):
        norm_copies.append(
            send(
                norm_box.at[ctx], norm_box.at[ctx], norm_ss.at[step], norm_rs.at[step],
                (dp, lax.rem(ctx + step, 16)),
            )
        )
    for copy in norm_copies:
        copy.wait()
    total_sq = jnp.sum(jnp.sum(norm_box[...], axis=0), axis=(0, 1), keepdims=True)
    factor = scale_total / (jnp.sqrt(total_sq) + gamma_floor)
    factor = jnp.broadcast_to(factor, (8, 128))
    fac_out[...] = factor
    send(fac_out, fac_in, pair_ss.at[4], pair_rs.at[4], twin).wait()
    half_copy.wait()
    mixed = acc[near_rows, :] * factor[0:1, 0:1] + half_in[...] * fac_in[0:1, 0:1]
    for place in range(CHIPS):
        r, w = (place % 8) * 16, (place // 8) * FEAT
        rs_out[place] = mixed[r : r + 16, w : w + FEAT].astype(BF16)
    rs_copies = []
    for step in range(1, CHIPS):
        other = lax.rem(chip + step, CHIPS)
        rs_copies.append(
            send(
                rs_out.at[other], rs_in.at[chip], rs_ss.at[step], rs_rs.at[step],
                (other * 2 + core, ctx),
            )
        )
    rs_in[chip] = rs_out[chip]
    for copy in rs_copies:
        copy.wait()
    piece = rs_in[0].astype(F32)
    for place in range(1, CHIPS):
        piece = piece + rs_in[place].astype(F32)
    ag[chip] = piece.astype(BF16)
    ag_copies = []
    for step in range(1, CHIPS):
        other = lax.rem(chip + step, CHIPS)
        ag_copies.append(
            send(
                ag.at[chip], ag.at[chip], ag_ss.at[step], ag_rs.at[step],
                (other * 2 + core, ctx),
            )
        )
    for copy in ag_copies:
        copy.wait()
    last = send(ag, ag_far, pair_ss.at[5], pair_rs.at[5], twin)
    for place in range(CHIPS):
        r, w = (place % 8) * 16, (place // 8) * FEAT
        rows = pl.ds(pl.multiple_of(core * TOK + r, 16), 16)
        out_ref[rows, pl.ds(w, FEAT)] = ag[place].astype(F32)
    last.wait()
    for place in range(CHIPS):
        r, w = (place % 8) * 16, (place // 8) * FEAT
        rows = pl.ds(pl.multiple_of((1 - core) * TOK + r, 16), 16)
        out_ref[rows, pl.ds(w, FEAT)] = ag_far[place].astype(F32)
    for copy in started + part_copies:
        copy.wait_send()


def on_device(hidden_in, query_states, key_states, value_states, out_grad, span_order):
    scale_total = math.sqrt(hidden_in.shape[2] * COLS / lax.axis_size("dp"))
    vmem = pl.BlockSpec(memory_space=pltpu.VMEM)
    dma = pltpu.SemaphoreType.DMA
    return pl.pallas_call(
        functools.partial(kernel, scale_total),
        name="clipped_grads",
        out_shape=jax.ShapeDtypeStruct((FEAT, COLS), F32),
        in_specs=[
            pl.BlockSpec(memory_space=pl.ANY), vmem, vmem, vmem, vmem,
            pl.BlockSpec(memory_space=pltpu.SMEM),
        ],
        out_specs=vmem,
        scratch_shapes=[
            pltpu.VMEM((NZ, 2 * TOK, FEAT), BF16),
            pltpu.VMEM((NZ, TOK, 2 * HEAD), BF16),
            pltpu.VMEM((2, TOK, 4 * HEAD), BF16),
            pltpu.VMEM((2, 4 * TOK, HEAD), BF16),
            pltpu.VMEM((8, 4 * HEAD), F32),
            pltpu.VMEM((8, 4 * HEAD), F32),
            pltpu.VMEM((NZ, TOK, 4 * HEAD), F32),
            pltpu.VMEM((NZ, TOK, 4 * HEAD), F32),
            pltpu.VMEM((NZ, TOK, 4 * HEAD), BF16),
            pltpu.VMEM((NZ, TOK, 2 * HEAD), BF16),
            pltpu.VMEM((NZ, TOK, 2 * HEAD), BF16),
            pltpu.VMEM((TOK, 2 * HEAD), BF16),
            pltpu.VMEM((TOK, 2 * HEAD), BF16),
            pltpu.VMEM((NZ, 2 * TOK, COLS), BF16),
            pltpu.VMEM((FEAT, COLS), F32),
            pltpu.VMEM((16, 8, 128), F32),
            pltpu.VMEM((TOK, COLS), F32),
            pltpu.VMEM((8, 128), F32),
            pltpu.VMEM((8, 128), F32),
            pltpu.VMEM((CHIPS, 16, FEAT), BF16),
            pltpu.VMEM((CHIPS, 16, FEAT), BF16),
            pltpu.VMEM((CHIPS, 16, FEAT), BF16),
            pltpu.VMEM((CHIPS, 16, FEAT), BF16),
            dma((16,)), dma((16,)),
            dma((4, 2, 5)), dma((4, 2, 5)),
            dma((6,)), dma((6,)),
            dma((4, 8)), dma((4, 8)),
            dma((8,)), dma((8,)),
            dma((16,)), dma((16,)),
            dma((16,)), dma((16,)),
            dma((16,)), dma((16,)),
            dma,
        ],
        compiler_params=pltpu.CompilerParams(
            collective_id=0, has_side_effects=True, vmem_limit_bytes=48 << 20
        ),
    )(hidden_in, query_states, key_states, value_states, out_grad, span_order)


def solution(mesh):
    return jax.shard_map(
        on_device,
        mesh=mesh,
        in_specs=(
            P("dp", "ctx", None),
            P("dp", "ctx", None),
            P("dp", "ctx", None),
            P("dp", "ctx", None),
            P("dp", "ctx", None),
            P("dp", None),
        ),
        out_specs=P("ctx", None),
        check_vma=False,
    )
```

time: 791 us -> 137 us (0.17)
  waiting for transfers between devices: 456 us -> 0 us
  starting transfers between devices: 170 us -> 0 us
  Pallas kernels: 0 us -> 131 us
  blocking collectives: 113 us -> 0 us
  matrix products: 18.8 us -> 0 us
  between operations: 14.3 us -> 0.02 us
    psum x1 -> x0, waiting for transfers between devices: 304 us -> none  [on_device(): return lax.psum(block_grad * factor, 'dp')]
    ppermute x64 -> x0, starting transfers between devices: 170 us -> none  [shifted(): return lax.ppermute(block, axis, route)]
    pallas_call x0 -> x1, Pallas kernels: none -> 131 us  [on_device(): pl.pallas_call(functools.partial(kernel, scale_total), name='clipped_grad...]
    all_gather x1 -> x0, waiting for transfers between devices: 89.5 us -> none  [on_device(): lax.all_gather(local_grads, 'ctx', axis=0, tiled=True)]
    all_gather x2 -> x0, blocking collectives: 66.2 us -> none  [the longest x1 38.4 us: on_device(): key_block = lax.all_gather(local_keys, 'ctx', axis=0, tiled=True)]
    ppermute x64 -> x0, waiting for transfers between devices: 62 us -> none  [shifted(): return lax.ppermute(block, axis, route)]
    psum x1 -> x0, blocking collectives: 26.9 us -> none  [on_device(): total_sq = lax.psum(jnp.sum(block_grad * block_grad), 'ctx')]
    all_to_all x1 -> x0, blocking collectives: 20.1 us -> none  [on_device(): lax.all_to_all(hidden_in[0], 'ctx', split_axis=1, concat_axis=0, tiled=True)]
  transfers between devices with their start and end apart: 66 -> 0, of which waited for: 32 -> 0; matrix products, arithmetic and copies ran while one was open for 3% -> 0% of each run, Pallas kernels for 0% -> 0%
where the time goes in v1:
time: 137 us
  Pallas kernels  131 us (96%)
  local copies, waits for them, and re-layouts  5.87 us (4%)
    pallas_call x1, Pallas kernels, on_device(): pl.pallas_call(functools.partial(kernel, scale_total), name='clipped_grad...  131 us
    unnamed x13, local copies, waits for them, and re-layouts  5.87 us

profile of v1, /device:TPU:1, one launch (start us, length us, event | category | flops | bytes accessed | tf_op | source)
XLA Modules:
  0.0 136.7 jit_solution(6410058756909611003)
XLA Ops:
  0.0 0.0 copy-start
  0.0 1.2 copy-done
  1.2 0.0 copy-start.1
  1.2 0.8 copy-done.1
  2.1 0.0 copy-start.2
  2.1 0.8 copy-done.2
  2.9 0.0 copy-start.3
  2.9 0.8 copy-done.3
  3.7 0.0 copy-start.4
  3.7 0.8 copy-done.4
  4.4 0.0 copy-start.5
  4.4 0.7 copy-done.5
  5.1 130.9 %clipped_grads.1 = f32[256,512]{1,0:T(8,128)S(1)} custom-call(bf16[1,128,4096]{2,1,0:T(8,128)(2,1)S(1)} %copy-done, bf16[1,128,256]{2,1,0:T(8,128)(2,1)S(1)} %copy-done.1, bf16[1,128,128]{2,1,0:T(8,128)(2,1)S(1)} %copy-done.3, bf16[1,128,128]{2,1,0:T(8,128)(2,1)S(1)} %copy-done.4, bf16[1,128,256]{2,1,0:T(8,128)(2,1)S(1)} %copy-done.2, s32[1,32]{1,0:T(1,128)S(1)} %copy-done.5), custom_call_target="tpu_custom_call" | custom-call | tf_op jit(solution)/shard_map/clipped_grads/pallas_call | solution.py:432
  135.9 0.8 copy.8
Async XLA Ops:
  0.0 1.2 copy-start
  1.2 0.8 copy-start.1
  2.1 0.8 copy-start.2
  2.9 0.8 copy-start.3
  3.7 0.8 copy-start.4
  4.4 0.7 copy-start.5

commit v2 on v1

v2 whole, which is shorter than its diff:
```python
import functools
import math

import jax
import jax.numpy as jnp
from jax import lax
from jax.experimental import pallas as pl
from jax.experimental.pallas import tpu as pltpu
from jax.sharding import PartitionSpec as P

MESH = pl.DeviceIdType.MESH
F32 = jnp.float32
BF16 = jnp.bfloat16

masked_fill = -1e30
gamma_floor = 0.01

TOK = 128
HEAD = 128
SPAN = 64
NZ = 8
FEAT = 256
COLS = 512
CHIPS = 16


def aligned(index, size):
    return pl.ds(pl.multiple_of(index * size, size), size)


def contract(left, right, left_dim, right_dim):
    return lax.dot_general(
        left, right, (((left_dim,), (right_dim,)), ((), ())), preferred_element_type=F32
    )


class Sent:
    def __init__(self, copy):
        self.copy = copy
        self.open_send = self.open_recv = True
        copy.start()

    def wait_recv(self):
        if self.open_recv:
            self.copy.wait_recv()
        self.open_recv = False

    def wait_send(self):
        if self.open_send:
            self.copy.wait_send()
        self.open_send = False


def kernel(
    scale_total,
    h_ref,
    q_ref,
    k_ref,
    v_ref,
    do_ref,
    span_ref,
    out_ref,
    hid,
    raw,
    keys,
    keys_t,
    values,
    queries,
    douts,
    expo,
    dprob,
    tops,
    key_acc,
    value_acc,
    grads,
    acc,
    norm_box,
    norm_far,
    half_in,
    rs_out,
    rs_in,
    ag,
    ag_far,
    spans,
    slots,
    hid_ss,
    hid_rs,
    ring_ss,
    ring_rs,
    twin_ss,
    twin_rs,
    fwd_ss,
    fwd_rs,
    norm_ss,
    norm_rs,
    rs_ss,
    rs_rs,
    ag_ss,
    ag_rs,
    own_sem,
):
    dp = lax.axis_index("dp")
    ctx = lax.axis_index("ctx")
    z = ctx // 2
    yl = lax.rem(ctx, 2)
    core = lax.rem(dp, 2)
    chip = dp // 2
    inv_scale = 1.0 / math.sqrt(HEAD)

    def zed(step):
        return lax.rem(z + step + NZ, NZ)

    up = (dp, zed(1) * 2 + yl)
    down = (dp, zed(-1) * 2 + yl)
    pair = (dp, z * 2 + (1 - yl))
    far_dp = chip * 2 + (1 - core)
    twin = (far_dp, ctx)

    def ctx_peer(step):
        return lax.rem(ctx + step, 16)

    def chip_peer(step):
        return lax.rem(chip // 4 + step // 4, 4) * 4 + lax.rem(chip + step % 4, 4)

    started = []

    def send(src, dst, ss, rs, device):
        copy = Sent(
            pltpu.make_async_remote_copy(
                src_ref=src, dst_ref=dst, send_sem=ss, recv_sem=rs,
                device_id=device, device_id_type=MESH,
            )
        )
        started.append(copy)
        return copy

    def finish():
        for copy in started:
            copy.wait_recv()
            copy.wait_send()

    barrier = pltpu.get_barrier_semaphore()
    for step in range(1, 16):
        for device in (
            (dp, ctx_peer(step)),
            (far_dp, ctx_peer(step)),
            (chip_peer(step) * 2 + core, ctx),
        ):
            pl.semaphore_signal(barrier, inc=1, device_id=device, device_id_type=MESH)
    pl.semaphore_signal(barrier, inc=1, device_id=twin, device_id_type=MESH)

    mine = aligned(ctx, TOK)
    loads = [pltpu.make_async_copy(span_ref, spans, own_sem.at[8])]
    for n, (ref, start, width) in enumerate(
        [(k_ref, 0, 128), (v_ref, 128, 128), (q_ref, 256, 256), (do_ref, 512, 256)]
    ):
        for s in range(2):
            loads.append(
                pltpu.make_async_copy(
                    ref.at[0, pl.ds(s * SPAN, SPAN)],
                    raw.at[2 * ctx + s, :, pl.ds(start, width)],
                    own_sem.at[2 * n + s],
                )
            )
    for load in loads:
        load.start()
    for load in loads:
        load.wait()
    pl.semaphore_wait(barrier, 46)

    def ring_send(lane, step, view_up, view_down):
        return (
            send(view_up, view_up, ring_ss.at[lane, 0, step], ring_rs.at[lane, 0, step], up),
            send(view_down, view_down, ring_ss.at[lane, 1, step], ring_rs.at[lane, 1, step], down),
        )

    def forward(lane, place, block_z, columns):
        view = raw.at[pl.ds(block_z * 4 + yl * 2, 2), :, columns]
        return send(view, view, fwd_ss.at[lane, place], fwd_rs.at[lane, place], pair)

    forwards = []

    def z_first(lane, start, width):
        columns = pl.ds(start, width)
        half = width // 2

        def views(step):
            if step < 4:
                return (
                    raw.at[pl.ds(zed(1 - step) * 4 + yl * 2, 2), :, columns],
                    raw.at[pl.ds(zed(step - 1) * 4 + yl * 2, 2), :, columns],
                )
            return (
                raw.at[pl.ds(zed(-3) * 4 + yl * 2, 2), :, pl.ds(start, half)],
                raw.at[pl.ds(zed(3) * 4 + yl * 2, 2), :, pl.ds(start + half, half)],
            )

        copies = ring_send(lane, 1, *views(1))
        forwards.append(forward(lane, 0, z, columns))
        yield
        for step in range(1, 5):
            for copy in copies:
                copy.wait_recv()
            if step < 4:
                copies = ring_send(lane, step + 1, *views(step + 1))
                forwards.append(forward(lane, 2 * step - 1, zed(-step), columns))
                forwards.append(forward(lane, 2 * step, zed(step), columns))
            else:
                forwards.append(forward(lane, 7, zed(4), columns))
            yield

    def y_first(lane, start, width):
        columns = pl.ds(start, width)
        exchange = forward(lane, 0, z, columns)
        yield

        def views(step):
            if step < 4:
                return (
                    raw.at[pl.ds(zed(1 - step) * 4, 4), :, columns],
                    raw.at[pl.ds(zed(step - 1) * 4, 4), :, columns],
                )
            return (
                raw.at[pl.ds(zed(-3) * 4, 2), :, columns],
                raw.at[pl.ds(zed(3) * 4 + 2, 2), :, columns],
            )

        exchange.wait_recv()
        copies = ring_send(lane, 1, *views(1))
        yield
        for step in range(1, 5):
            for copy in copies:
                copy.wait_recv()
            if step < 4:
                copies = ring_send(lane, step + 1, *views(step + 1))
            yield

    lanes = [y_first(0, 0, 256), z_first(1, 256, 256), z_first(2, 512, 256)]
    for lane in lanes:
        next(lane)
    next(lanes[0])

    own_copy = pltpu.make_async_copy(
        h_ref.at[0, :, aligned(ctx, FEAT)], hid.at[mine, :], own_sem.at[9]
    )
    own_copy.start()

    def find_slot(block, carry):
        slot = jnp.int32(0)
        for s in range(32):
            slot = jnp.where(spans[0, s] == block, jnp.int32(s), slot)
        slots[block] = slot
        return carry

    lax.fori_loop(0, 32, find_slot, 0)
    for step in range(1, 5):
        for lane in lanes:
            next(lane)
    for copy in forwards:
        copy.wait_recv()

    hid_copies = []
    for ahead in [8, 9, 7, 10, 6, 11, 5, 12, 4, 13, 3, 14, 2, 15, 1]:
        peer = ctx_peer(ahead)
        hid_copies.append(
            send(
                h_ref.at[0, :, aligned(peer, FEAT)], hid.at[mine, :],
                hid_ss.at[ahead], hid_rs.at[ahead], (dp, peer),
            )
        )

    def place_block(block, carry):
        rows = raw[slots[block]]
        keys[aligned(block, SPAN), :] = rows[:, :128]
        values[aligned(block, SPAN), :] = rows[:, 128:256]
        tile = block // 4
        for h in range(2):
            into = aligned(h * 4 + lax.rem(block, 4), SPAN)
            queries[tile, into, :] = rows[:, 256 + h * 128 : 384 + h * 128]
            douts[tile, into, :] = rows[:, 512 + h * 128 : 640 + h * 128]
        return carry

    lax.fori_loop(0, 32, place_block, 0)
    keys_t[...] = keys[...].T
    key_acc[...] = jnp.zeros_like(key_acc)
    value_acc[...] = jnp.zeros_like(value_acc)

    to_log2 = inv_scale * math.log2(math.e)

    def query_tile(tile, carry):
        query = queries[tile]
        dout = douts[tile]

        def totals(block, running, diagonal=False):
            top, total, dot = running
            rows = aligned(block, 256)
            scores = contract(keys[rows, :], query, 1, 1) * to_log2
            if diagonal:
                key_at = lax.broadcasted_iota(jnp.int32, (256, 512), 0)
                query_at = lax.rem(lax.broadcasted_iota(jnp.int32, (256, 512), 1), 256)
                scores = jnp.where(key_at <= query_at, scores, masked_fill)
            probs = contract(values[rows, :], dout, 1, 1)
            here = jnp.max(scores, axis=0, keepdims=True)
            weights = jnp.exp2(scores - here)
            expo[rows, :] = weights
            dprob[rows, :] = probs
            tops[block] = jnp.broadcast_to(here, (8, 512))
            new_top = jnp.maximum(top, here)
            old, new = jnp.exp2(top - new_top), jnp.exp2(here - new_top)
            total = old * total + new * jnp.sum(weights, axis=0, keepdims=True)
            dot = old * dot + new * jnp.sum(weights * probs, axis=0, keepdims=True)
            return new_top, total, dot

        running = (
            jnp.full((1, 512), masked_fill, F32),
            jnp.zeros((1, 512), F32),
            jnp.zeros((1, 512), F32),
        )
        running = totals(tile, running, True)
        top, total, dot = lax.fori_loop(0, tile, totals, running)
        log_total = top + jnp.log2(total)
        row_delta = dot / total

        def gradients(block, query_sum):
            rows = aligned(block, 256)
            probs = expo[rows, :] * jnp.exp2(tops[block][0:1] - log_total)
            scores_low = (probs * (dprob[rows, :] - row_delta)).astype(BF16)
            value_acc[rows, :] += jnp.dot(
                probs.astype(BF16), dout, preferred_element_type=F32
            )
            key_acc[rows, :] += jnp.dot(scores_low, query, preferred_element_type=F32)
            return query_sum + jnp.dot(keys_t[:, rows], scores_low, preferred_element_type=F32)

        query_sum = lax.fori_loop(0, tile + 1, gradients, jnp.zeros((128, 512), F32))
        query_sum = (query_sum.T * inv_scale).astype(BF16)
        rows = pl.ds(tile * 4, 4)
        grads[rows, :, :128] = query_sum[:256].reshape(4, SPAN, 128)
        grads[rows, :, 128:256] = query_sum[256:].reshape(4, SPAN, 128)
        return carry

    lax.fori_loop(0, 8, query_tile, 0)
    grads[:, :, 256:384] = (key_acc[...] * inv_scale).astype(BF16).reshape(32, SPAN, 128)
    grads[:, :, 384:] = value_acc[...].astype(BF16).reshape(32, SPAN, 128)

    own_copy.wait()
    for copy in hid_copies:
        copy.wait_recv()

    for block in range(NZ):
        part = jnp.concatenate(
            [grads[spans[0, block * 4 + s]] for s in range(4)], axis=0
        )
        part = contract(hid[block * 256 : (block + 1) * 256, :], part, 0, 0)
        if block == 0:
            acc[...] = part
        else:
            acc[...] += part

    near_rows = aligned(core, TOK)
    half_copy = send(
        acc.at[aligned(1 - core, TOK)], half_in, twin_ss.at[0], twin_rs.at[0], twin
    )
    whole = acc[...]
    squares = jnp.sum((whole * whole).reshape(32, 8, COLS), axis=0)
    norm_box[ctx] = (
        squares[:, :128] + squares[:, 128:256] + squares[:, 256:384] + squares[:, 384:]
    )
    norm_copies = []
    for ahead in range(16):
        place = norm_box.at[ctx]
        if ahead:
            norm_copies.append(
                send(
                    place, place, norm_ss.at[0, ahead], norm_rs.at[0, ahead],
                    (dp, ctx_peer(ahead)),
                )
            )
        norm_copies.append(
            send(
                place, norm_far.at[ctx], norm_ss.at[1, ahead], norm_rs.at[1, ahead],
                (far_dp, ctx_peer(ahead)),
            )
        )
    for copy in norm_copies:
        copy.wait_recv()

    def factor_of(box):
        total_sq = jnp.sum(jnp.sum(box[...], axis=0), axis=(0, 1), keepdims=True)
        return scale_total / (jnp.sqrt(total_sq) + gamma_floor)

    near_factor = factor_of(norm_box)
    far_factor = factor_of(norm_far)
    half_copy.wait_recv()
    mixed = acc[near_rows, :] * near_factor + half_in[...] * far_factor
    for place in range(CHIPS):
        r, w = (place % 8) * 16, (place // 8) * FEAT
        rs_out[place] = mixed[r : r + 16, w : w + FEAT].astype(BF16)

    chip_order = [10, 8, 2, 9, 11, 6, 14, 5, 7, 13, 15, 4, 12, 1, 3]
    rs_copies = []
    for step in chip_order:
        other = chip_peer(step)
        rs_copies.append(
            send(
                rs_out.at[other], rs_in.at[chip], rs_ss.at[step], rs_rs.at[step],
                (other * 2 + core, ctx),
            )
        )
    rs_in[chip] = rs_out[chip]
    for copy in rs_copies:
        copy.wait_recv()

    piece = rs_in[0].astype(F32)
    for place in range(1, CHIPS):
        piece = piece + rs_in[place].astype(F32)
    ag[chip] = piece.astype(BF16)
    ag_copies = []
    for step in chip_order:
        other = chip_peer(step)
        ag_copies.append(
            send(
                ag.at[chip], ag.at[chip], ag_ss.at[step], ag_rs.at[step],
                (other * 2 + core, ctx),
            )
        )
    for copy in ag_copies:
        copy.wait_recv()

    last = send(ag, ag_far, twin_ss.at[1], twin_rs.at[1], twin)
    for place in range(CHIPS):
        r, w = (place % 8) * 16, (place // 8) * FEAT
        rows = pl.ds(pl.multiple_of(core * TOK + r, 16), 16)
        out_ref[rows, pl.ds(w, FEAT)] = ag[place].astype(F32)
    last.wait_recv()
    for place in range(CHIPS):
        r, w = (place % 8) * 16, (place // 8) * FEAT
        rows = pl.ds(pl.multiple_of((1 - core) * TOK + r, 16), 16)
        out_ref[rows, pl.ds(w, FEAT)] = ag_far[place].astype(F32)
    finish()


def on_device(hidden_in, query_states, key_states, value_states, out_grad, span_order):
    scale_total = math.sqrt(hidden_in.shape[2] * COLS / lax.axis_size("dp"))
    vmem = pl.BlockSpec(memory_space=pltpu.VMEM)
    dma = pltpu.SemaphoreType.DMA
    return pl.pallas_call(
        functools.partial(kernel, scale_total),
        name="clipped_grads",
        out_shape=jax.ShapeDtypeStruct((FEAT, COLS), F32),
        in_specs=[pl.BlockSpec(memory_space=pl.ANY)] * 6,
        out_specs=vmem,
        scratch_shapes=[
            pltpu.VMEM((16 * TOK, FEAT), BF16),
            pltpu.VMEM((32, SPAN, 6 * HEAD), BF16),
            pltpu.VMEM((16 * TOK, HEAD), BF16),
            pltpu.VMEM((HEAD, 16 * TOK), BF16),
            pltpu.VMEM((16 * TOK, HEAD), BF16),
            pltpu.VMEM((8, 512, HEAD), BF16),
            pltpu.VMEM((8, 512, HEAD), BF16),
            pltpu.VMEM((16 * TOK, 512), F32),
            pltpu.VMEM((16 * TOK, 512), F32),
            pltpu.VMEM((8, 8, 512), F32),
            pltpu.VMEM((16 * TOK, HEAD), F32),
            pltpu.VMEM((16 * TOK, HEAD), F32),
            pltpu.VMEM((32, SPAN, COLS), BF16),
            pltpu.VMEM((FEAT, COLS), F32),
            pltpu.VMEM((16, 8, 128), F32),
            pltpu.VMEM((16, 8, 128), F32),
            pltpu.VMEM((TOK, COLS), F32),
            pltpu.VMEM((CHIPS, 16, FEAT), BF16),
            pltpu.VMEM((CHIPS, 16, FEAT), BF16),
            pltpu.VMEM((CHIPS, 16, FEAT), BF16),
            pltpu.VMEM((CHIPS, 16, FEAT), BF16),
            pltpu.SMEM((1, 32), jnp.int32),
            pltpu.SMEM((32,), jnp.int32),
            dma((16,)), dma((16,)),
            dma((3, 2, 5)), dma((3, 2, 5)),
            dma((2,)), dma((2,)),
            dma((3, 8)), dma((3, 8)),
            dma((2, 16)), dma((2, 16)),
            dma((16,)), dma((16,)),
            dma((16,)), dma((16,)),
            dma((10,)),
        ],
        compiler_params=pltpu.CompilerParams(
            collective_id=0, has_side_effects=True, vmem_limit_bytes=62 << 20
        ),
    )(hidden_in, query_states, key_states, value_states, out_grad, span_order)


def solution(mesh):
    return jax.shard_map(
        on_device,
        mesh=mesh,
        in_specs=(
            P("dp", "ctx", None),
            P("dp", "ctx", None),
            P("dp", "ctx", None),
            P("dp", "ctx", None),
            P("dp", "ctx", None),
            P("dp", None),
        ),
        out_specs=P("ctx", None),
        check_vma=False,
    )
```

time: 137 us -> 102 us (0.74)
  Pallas kernels: 131 us -> 99.5 us
  local copies, waits for them, and re-layouts: 5.87 us -> 1.87 us
    pallas_call x1, Pallas kernels: 131 us -> 99.5 us  [on_device(): pl.pallas_call(functools.partial(kernel, scale_total), name='clipped_grad...]
    unnamed x13 -> x1, local copies, waits for them, and re-layouts: 5.87 us -> 1.87 us
where the time goes in v2:
time: 102 us; the launch traced here: 101 us
  Pallas kernels  99.5 us (98%)
  local copies, waits for them, and re-layouts  1.87 us (2%)
    pallas_call x1, Pallas kernels, on_device(): pl.pallas_call(functools.partial(kernel, scale_total), name='clipped_grad...  99.5 us

profile of v2, /device:TPU:1, one launch (start us, length us, event | category | flops | bytes accessed | tf_op | source)
XLA Modules:
  0.0 101.4 jit_solution(1400237861107121889)
XLA Ops:
  0.0 99.5 %clipped_grads.1 = f32[256,512]{1,0:T(8,128)} custom-call(bf16[1,128,4096]{2,1,0:T(8,128)(2,1)} %h_ref.1, bf16[1,128,256]{2,1,0:T(8,128)(2,1)} %q_ref.1, bf16[1,128,128]{2,1,0:T(8,128)(2,1)} %k_ref.1, bf16[1,128,128]{2,1,0:T(8,128)(2,1)} %v_ref.1, bf16[1,128,256]{2,1,0:T(8,128)(2,1)} %do_ref.1, s32[1,32]{1,0:T(1,128)} %span_ref.1), custom_call_target="tpu_custom_call" | custom-call | tf_op jit(solution)/shard_map/clipped_grads/pallas_call | solution.py:446
  99.5 1.9 %copy.8 = f32[256,512]{1,0:T(8,128)} copy(f32[256,512]{1,0:T(8,128)} %clipped_grads.1) | data formatting | bytes 1048576

commit v3 on v2

--- a/solution.py
+++ b/solution.py
@@ -72,11 +72,11 @@
     tops,
     key_acc,
     value_acc,
+    query_acc,
     grads,
     acc,
     norm_box,
-    norm_far,
-    half_in,
+    fac,
     rs_out,
     rs_in,
     ag,
@@ -93,6 +93,8 @@
     fwd_rs,
     norm_ss,
     norm_rs,
+    fac_ss,
+    fac_rs,
     rs_ss,
     rs_rs,
     ag_ss,
@@ -113,8 +115,7 @@
     up = (dp, zed(1) * 2 + yl)
     down = (dp, zed(-1) * 2 + yl)
     pair = (dp, z * 2 + (1 - yl))
-    far_dp = chip * 2 + (1 - core)
-    twin = (far_dp, ctx)
+    twin = (chip * 2 + (1 - core), ctx)
 
     def ctx_peer(step):
         return lax.rem(ctx + step, 16)
@@ -122,6 +123,7 @@
     def chip_peer(step):
         return lax.rem(chip // 4 + step // 4, 4) * 4 + lax.rem(chip + step % 4, 4)
 
+    ctx_order = [8, 9, 7, 10, 6, 11, 5, 12, 4, 13, 3, 14, 2, 15, 1]
     started = []
 
     def send(src, dst, ss, rs, device):
@@ -143,8 +145,8 @@
     for step in range(1, 16):
         for device in (
             (dp, ctx_peer(step)),
-            (far_dp, ctx_peer(step)),
-            (chip_peer(step) * 2 + core, ctx),
+            (chip_peer(step) * 2, ctx),
+            (chip_peer(step) * 2 + 1, ctx),
         ):
             pl.semaphore_signal(barrier, inc=1, device_id=device, device_id_type=MESH)
     pl.semaphore_signal(barrier, inc=1, device_id=twin, device_id_type=MESH)
@@ -182,7 +184,6 @@
 
     def z_first(lane, start, width):
         columns = pl.ds(start, width)
-        half = width // 2
 
         def views(step):
             if step < 4:
@@ -191,8 +192,8 @@
                     raw.at[pl.ds(zed(step - 1) * 4 + yl * 2, 2), :, columns],
                 )
             return (
-                raw.at[pl.ds(zed(-3) * 4 + yl * 2, 2), :, pl.ds(start, half)],
-                raw.at[pl.ds(zed(3) * 4 + yl * 2, 2), :, pl.ds(start + half, half)],
+                raw.at[zed(-3) * 4 + yl * 2, :, columns],
+                raw.at[zed(3) * 4 + yl * 2 + 1, :, columns],
             )
 
         copies = ring_send(lane, 1, *views(1))
@@ -238,7 +239,8 @@
     lanes = [y_first(0, 0, 256), z_first(1, 256, 256), z_first(2, 512, 256)]
     for lane in lanes:
         next(lane)
-    next(lanes[0])
+    for lane in lanes[:1]:
+        next(lane)
 
     own_copy = pltpu.make_async_copy(
         h_ref.at[0, :, aligned(ctx, FEAT)], hid.at[mine, :], own_sem.at[9]
@@ -253,21 +255,27 @@
         return carry
 
     lax.fori_loop(0, 32, find_slot, 0)
+    hid_copies = []
+
+    def send_features(aheads):
+        for ahead in aheads:
+            peer = ctx_peer(ahead)
+            hid_copies.append(
+                send(
+                    h_ref.at[0, :, aligned(peer, FEAT)], hid.at[mine, :],
+                    hid_ss.at[ahead], hid_rs.at[ahead], (dp, peer),
+                )
+            )
+
+    early = {1: [2, 14], 2: [3, 15], 3: [1]}
     for step in range(1, 5):
         for lane in lanes:
             next(lane)
+        send_features(early.get(step, []))
     for copy in forwards:
         copy.wait_recv()
 
-    hid_copies = []
-    for ahead in [8, 9, 7, 10, 6, 11, 5, 12, 4, 13, 3, 14, 2, 15, 1]:
-        peer = ctx_peer(ahead)
-        hid_copies.append(
-            send(
-                h_ref.at[0, :, aligned(peer, FEAT)], hid.at[mine, :],
-                hid_ss.at[ahead], hid_rs.at[ahead], (dp, peer),
-            )
-        )
+    send_features([8, 9, 7, 10, 6, 11, 5, 12, 4, 13])
 
     def place_block(block, carry):
         rows = raw[slots[block]]
@@ -282,63 +290,79 @@
 
     lax.fori_loop(0, 32, place_block, 0)
     keys_t[...] = keys[...].T
-    key_acc[...] = jnp.zeros_like(key_acc)
-    value_acc[...] = jnp.zeros_like(value_acc)
 
     to_log2 = inv_scale * math.log2(math.e)
 
-    def query_tile(tile, carry):
-        query = queries[tile]
-        dout = douts[tile]
-
-        def totals(block, running, diagonal=False):
-            top, total, dot = running
-            rows = aligned(block, 256)
+    def totals(tile, block, head, running):
+        top, total, dot = running
+        lanes = pl.ds(head * 256, 256)
+        query, dout = queries[tile, lanes, :], douts[tile, lanes, :]
+        for part in range(2):
+            rows = pl.ds(block * 256 + part * 128, 128)
             scores = contract(keys[rows, :], query, 1, 1) * to_log2
-            if diagonal:
-                key_at = lax.broadcasted_iota(jnp.int32, (256, 512), 0)
-                query_at = lax.rem(lax.broadcasted_iota(jnp.int32, (256, 512), 1), 256)
+            if block == tile:
+                key_at = lax.broadcasted_iota(jnp.int32, (128, 256), 0) + part * 128
+                query_at = lax.broadcasted_iota(jnp.int32, (128, 256), 1)
                 scores = jnp.where(key_at <= query_at, scores, masked_fill)
             probs = contract(values[rows, :], dout, 1, 1)
             here = jnp.max(scores, axis=0, keepdims=True)
             weights = jnp.exp2(scores - here)
-            expo[rows, :] = weights
-            dprob[rows, :] = probs
-            tops[block] = jnp.broadcast_to(here, (8, 512))
+            expo[rows, lanes] = weights
+            dprob[rows, lanes] = probs
+            tops[block * 2 + part, :, lanes] = jnp.broadcast_to(here, (8, 256))
             new_top = jnp.maximum(top, here)
             old, new = jnp.exp2(top - new_top), jnp.exp2(here - new_top)
             total = old * total + new * jnp.sum(weights, axis=0, keepdims=True)
             dot = old * dot + new * jnp.sum(weights * probs, axis=0, keepdims=True)
-            return new_top, total, dot
-
-        running = (
-            jnp.full((1, 512), masked_fill, F32),
-            jnp.zeros((1, 512), F32),
-            jnp.zeros((1, 512), F32),
+            top = new_top
+        return top, total, dot
+
+    def gradients(tile, block, log_total, row_delta):
+        probs = jnp.concatenate(
+            [
+                expo[pl.ds(block * 256 + part * 128, 128), :]
+                * jnp.exp2(tops[block * 2 + part, 0:1, :] - log_total)
+                for part in range(2)
+            ],
+            axis=0,
         )
-        running = totals(tile, running, True)
-        top, total, dot = lax.fori_loop(0, tile, totals, running)
+        rows = pl.ds(block * 256, 256)
+        scores_low = (probs * (dprob[rows, :] - row_delta)).astype(BF16)
+        value_add = jnp.dot(probs.astype(BF16), douts[tile], preferred_element_type=F32)
+        key_add = jnp.dot(scores_low, queries[tile], preferred_element_type=F32)
+        if tile == block:
+            value_acc[rows, :] = value_add
+            key_acc[rows, :] = key_add
+        else:
+            value_acc[rows, :] += value_add
+            key_acc[rows, :] += key_add
+        return jnp.dot(keys_t[:, rows], scores_low, preferred_element_type=F32)
+
+    for tile in range(8):
+        heads = []
+        for head in range(2):
+            running = (
+                jnp.full((1, 256), masked_fill, F32),
+                jnp.zeros((1, 256), F32),
+                jnp.zeros((1, 256), F32),
+            )
+            for block in [tile, *range(tile)]:
+                running = totals(tile, block, head, running)
+            heads.append(running)
+        top, total, dot = (jnp.concatenate(both, axis=1) for both in zip(*heads))
         log_total = top + jnp.log2(total)
         row_delta = dot / total
-
-        def gradients(block, query_sum):
-            rows = aligned(block, 256)
-            probs = expo[rows, :] * jnp.exp2(tops[block][0:1] - log_total)
-            scores_low = (probs * (dprob[rows, :] - row_delta)).astype(BF16)
-            value_acc[rows, :] += jnp.dot(
-                probs.astype(BF16), dout, preferred_element_type=F32
-            )
-            key_acc[rows, :] += jnp.dot(scores_low, query, preferred_element_type=F32)
-            return query_sum + jnp.dot(keys_t[:, rows], scores_low, preferred_element_type=F32)
-
-        query_sum = lax.fori_loop(0, tile + 1, gradients, jnp.zeros((128, 512), F32))
-        query_sum = (query_sum.T * inv_scale).astype(BF16)
+        for block in range(tile + 1):
+            query_add = gradients(tile, block, log_total, row_delta)
+            if block == 0:
+                query_acc[...] = query_add
+            else:
+                query_acc[...] += query_add
+        query_sum = (query_acc[...].T * inv_scale).astype(BF16)
         rows = pl.ds(tile * 4, 4)
         grads[rows, :, :128] = query_sum[:256].reshape(4, SPAN, 128)
         grads[rows, :, 128:256] = query_sum[256:].reshape(4, SPAN, 128)
-        return carry
-
-    lax.fori_loop(0, 8, query_tile, 0)
+
     grads[:, :, 256:384] = (key_acc[...] * inv_scale).astype(BF16).reshape(32, SPAN, 128)
     grads[:, :, 384:] = value_acc[...].astype(BF16).reshape(32, SPAN, 128)
 
@@ -356,66 +380,64 @@
         else:
             acc[...] += part
 
-    near_rows = aligned(core, TOK)
-    half_copy = send(
-        acc.at[aligned(1 - core, TOK)], half_in, twin_ss.at[0], twin_rs.at[0], twin
-    )
     whole = acc[...]
     squares = jnp.sum((whole * whole).reshape(32, 8, COLS), axis=0)
     norm_box[ctx] = (
         squares[:, :128] + squares[:, 128:256] + squares[:, 256:384] + squares[:, 384:]
     )
     norm_copies = []
-    for ahead in range(16):
+    for ahead in ctx_order:
         place = norm_box.at[ctx]
-        if ahead:
-            norm_copies.append(
+        norm_copies.append(
+            send(place, place, norm_ss.at[ahead], norm_rs.at[ahead], (dp, ctx_peer(ahead)))
+        )
+
+    for place in range(32):
+        r, w = (place // 2) * 16, (place % 2) * FEAT
+        rs_out[place] = whole[r : r + 16, w : w + FEAT].astype(BF16)
+    chip_order = [10, 8, 2, 9, 11, 6, 14, 5, 7, 13, 15, 4, 12, 1, 3, 0]
+    rs_copies = []
+    for step in chip_order:
+        for side in range(2):
+            if step == 0 and side == 0:
+                continue
+            other = chip_peer(step) * 2 + lax.rem(core + side, 2)
+            rs_copies.append(
                 send(
-                    place, place, norm_ss.at[0, ahead], norm_rs.at[0, ahead],
-                    (dp, ctx_peer(ahead)),
+                    rs_out.at[other], rs_in.at[dp], rs_ss.at[step * 2 + side],
+                    rs_rs.at[step * 2 + side], (other, ctx),
                 )
             )
-        norm_copies.append(
-            send(
-                place, norm_far.at[ctx], norm_ss.at[1, ahead], norm_rs.at[1, ahead],
-                (far_dp, ctx_peer(ahead)),
-            )
-        )
+    rs_in[dp] = rs_out[dp]
     for copy in norm_copies:
         copy.wait_recv()
 
-    def factor_of(box):
-        total_sq = jnp.sum(jnp.sum(box[...], axis=0), axis=(0, 1), keepdims=True)
-        return scale_total / (jnp.sqrt(total_sq) + gamma_floor)
-
-    near_factor = factor_of(norm_box)
-    far_factor = factor_of(norm_far)
-    half_copy.wait_recv()
-    mixed = acc[near_rows, :] * near_factor + half_in[...] * far_factor
-    for place in range(CHIPS):
-        r, w = (place % 8) * 16, (place // 8) * FEAT
-        rs_out[place] = mixed[r : r + 16, w : w + FEAT].astype(BF16)
-
-    chip_order = [10, 8, 2, 9, 11, 6, 14, 5, 7, 13, 15, 4, 12, 1, 3]
-    rs_copies = []
+    total_sq = jnp.sum(jnp.sum(norm_box[...], axis=0), axis=(0, 1), keepdims=True)
+    factor = scale_total / (jnp.sqrt(total_sq) + gamma_floor)
+    fac[dp] = jnp.broadcast_to(factor, (8, 128))
+    fac_copies = []
     for step in chip_order:
-        other = chip_peer(step)
-        rs_copies.append(
-            send(
-                rs_out.at[other], rs_in.at[chip], rs_ss.at[step], rs_rs.at[step],
-                (other * 2 + core, ctx),
-            )
-        )
-    rs_in[chip] = rs_out[chip]
-    for copy in rs_copies:
+        for side in range(2):
+            if step == 0 and side == 0:
+                continue
+            other = chip_peer(step) * 2 + lax.rem(core + side, 2)
+            fac_copies.append(
+                send(
+                    fac.at[dp], fac.at[dp], fac_ss.at[step * 2 + side],
+                    fac_rs.at[step * 2 + side], (other, ctx),
+                )
+            )
+
+    for copy in rs_copies + fac_copies:
         copy.wait_recv()
 
-    piece = rs_in[0].astype(F32)
-    for place in range(1, CHIPS):
-        piece = piece + rs_in[place].astype(F32)
+    piece = jnp.zeros((16, FEAT), F32)
+    for place in range(32):
+        row = fac[place, 0:1, :]
+        piece += rs_in[place].astype(F32) * jnp.concatenate([row, row], axis=1)
     ag[chip] = piece.astype(BF16)
     ag_copies = []
-    for step in chip_order:
+    for step in chip_order[:-1]:
         other = chip_peer(step)
         ag_copies.append(
             send(
@@ -426,16 +448,12 @@
     for copy in ag_copies:
         copy.wait_recv()
 
-    last = send(ag, ag_far, twin_ss.at[1], twin_rs.at[1], twin)
+    last = send(ag, ag_far, twin_ss.at[0], twin_rs.at[0], twin)
     for place in range(CHIPS):
-        r, w = (place % 8) * 16, (place // 8) * FEAT
-        rows = pl.ds(pl.multiple_of(core * TOK + r, 16), 16)
-        out_ref[rows, pl.ds(w, FEAT)] = ag[place].astype(F32)
+        out_ref[place * 16 : place * 16 + 16, aligned(core, FEAT)] = ag[place].astype(F32)
     last.wait_recv()
     for place in range(CHIPS):
-        r, w = (place % 8) * 16, (place // 8) * FEAT
-        rows = pl.ds(pl.multiple_of((1 - core) * TOK + r, 16), 16)
-        out_ref[rows, pl.ds(w, FEAT)] = ag_far[place].astype(F32)
+        out_ref[place * 16 : place * 16 + 16, aligned(1 - core, FEAT)] = ag_far[place].astype(F32)
     finish()
 
 
@@ -459,26 +477,27 @@
             pltpu.VMEM((8, 512, HEAD), BF16),
             pltpu.VMEM((16 * TOK, 512), F32),
             pltpu.VMEM((16 * TOK, 512), F32),
-            pltpu.VMEM((8, 8, 512), F32),
+            pltpu.VMEM((16, 8, 512), F32),
             pltpu.VMEM((16 * TOK, HEAD), F32),
             pltpu.VMEM((16 * TOK, HEAD), F32),
+            pltpu.VMEM((HEAD, 512), F32),
             pltpu.VMEM((32, SPAN, COLS), BF16),
             pltpu.VMEM((FEAT, COLS), F32),
             pltpu.VMEM((16, 8, 128), F32),
-            pltpu.VMEM((16, 8, 128), F32),
-            pltpu.VMEM((TOK, COLS), F32),
-            pltpu.VMEM((CHIPS, 16, FEAT), BF16),
-            pltpu.VMEM((CHIPS, 16, FEAT), BF16),
+            pltpu.VMEM((32, 8, 128), F32),
+            pltpu.VMEM((32, 16, FEAT), BF16),
+            pltpu.VMEM((32, 16, FEAT), BF16),
             pltpu.VMEM((CHIPS, 16, FEAT), BF16),
             pltpu.VMEM((CHIPS, 16, FEAT), BF16),
             pltpu.SMEM((1, 32), jnp.int32),
             pltpu.SMEM((32,), jnp.int32),
             dma((16,)), dma((16,)),
-            dma((3, 2, 5)), dma((3, 2, 5)),
+            dma((6, 2, 5)), dma((6, 2, 5)),
             dma((2,)), dma((2,)),
-            dma((3, 8)), dma((3, 8)),
-            dma((2, 16)), dma((2, 16)),
+            dma((6, 8)), dma((6, 8)),
             dma((16,)), dma((16,)),
+            dma((32,)), dma((32,)),
+            dma((32,)), dma((32,)),
             dma((16,)), dma((16,)),
             dma((10,)),
         ],

time: 102 us -> 98.8 us (0.969)
  Pallas kernels: 99.5 us -> 96.6 us
    pallas_call x1, Pallas kernels: 99.5 us -> 96.6 us  [on_device(): pl.pallas_call(functools.partial(kernel, scale_total), name='clipped_grad...]
where the time goes in v3:
time: 98.8 us; the launch traced here: 98.5 us
  Pallas kernels  96.6 us (98%)
  local copies, waits for them, and re-layouts  1.87 us (2%)
    pallas_call x1, Pallas kernels, on_device(): pl.pallas_call(functools.partial(kernel, scale_total), name='clipped_grad...  96.6 us

profile of v3, /device:TPU:1, one launch (start us, length us, event | category | flops | bytes accessed | tf_op | source)
XLA Modules:
  0.0 98.5 jit_solution(10928739936349532912)
XLA Ops:
  0.0 96.6 %clipped_grads.1 = f32[256,512]{1,0:T(8,128)} custom-call(bf16[1,128,4096]{2,1,0:T(8,128)(2,1)} %h_ref.1, bf16[1,128,256]{2,1,0:T(8,128)(2,1)} %q_ref.1, bf16[1,128,128]{2,1,0:T(8,128)(2,1)} %k_ref.1, bf16[1,128,128]{2,1,0:T(8,128)(2,1)} %v_ref.1, bf16[1,128,256]{2,1,0:T(8,128)(2,1)} %do_ref.1, s32[1,32]{1,0:T(1,128)} %span_ref.1), custom_call_target="tpu_custom_call" | custom-call | tf_op jit(solution)/shard_map/clipped_grads/pallas_call | solution.py:464
  96.7 1.9 %copy.8 = f32[256,512]{1,0:T(8,128)} copy(f32[256,512]{1,0:T(8,128)} %clipped_grads.1) | data formatting | bytes 1048576

commit v4 on v3

--- a/solution.py
+++ b/solution.py
@@ -76,11 +76,11 @@
     grads,
     acc,
     norm_box,
-    fac,
+    norm_far,
+    half_in,
     rs_out,
     rs_in,
     ag,
-    ag_far,
     spans,
     slots,
     hid_ss,
@@ -93,8 +93,6 @@
     fwd_rs,
     norm_ss,
     norm_rs,
-    fac_ss,
-    fac_rs,
     rs_ss,
     rs_rs,
     ag_ss,
@@ -115,7 +113,8 @@
     up = (dp, zed(1) * 2 + yl)
     down = (dp, zed(-1) * 2 + yl)
     pair = (dp, z * 2 + (1 - yl))
-    twin = (chip * 2 + (1 - core), ctx)
+    far_dp = chip * 2 + (1 - core)
+    twin = (far_dp, ctx)
 
     def ctx_peer(step):
         return lax.rem(ctx + step, 16)
@@ -140,16 +139,6 @@
         for copy in started:
             copy.wait_recv()
             copy.wait_send()
-
-    barrier = pltpu.get_barrier_semaphore()
-    for step in range(1, 16):
-        for device in (
-            (dp, ctx_peer(step)),
-            (chip_peer(step) * 2, ctx),
-            (chip_peer(step) * 2 + 1, ctx),
-        ):
-            pl.semaphore_signal(barrier, inc=1, device_id=device, device_id_type=MESH)
-    pl.semaphore_signal(barrier, inc=1, device_id=twin, device_id_type=MESH)
 
     mine = aligned(ctx, TOK)
     loads = [pltpu.make_async_copy(span_ref, spans, own_sem.at[8])]
@@ -166,6 +155,16 @@
             )
     for load in loads:
         load.start()
+
+    barrier = pltpu.get_barrier_semaphore()
+    for step in ctx_order:
+        for device in (
+            (dp, ctx_peer(step)),
+            (far_dp, ctx_peer(step)),
+            (chip_peer(step) * 2 + core, ctx),
+        ):
+            pl.semaphore_signal(barrier, inc=1, device_id=device, device_id_type=MESH)
+    pl.semaphore_signal(barrier, inc=1, device_id=twin, device_id_type=MESH)
     for load in loads:
         load.wait()
     pl.semaphore_wait(barrier, 46)
@@ -267,7 +266,7 @@
                 )
             )
 
-    early = {1: [2, 14], 2: [3, 15], 3: [1]}
+    early = {3: [8], 4: [6, 10, 4, 12, 2, 14]}
     for step in range(1, 5):
         for lane in lanes:
             next(lane)
@@ -275,7 +274,7 @@
     for copy in forwards:
         copy.wait_recv()
 
-    send_features([8, 9, 7, 10, 6, 11, 5, 12, 4, 13])
+    send_features([9, 7, 11, 5, 13, 3, 15, 1])
 
     def place_block(block, carry):
         rows = raw[slots[block]]
@@ -380,64 +379,63 @@
         else:
             acc[...] += part
 
+    half_copy = send(
+        acc.at[:, aligned(1 - core, FEAT)], half_in, twin_ss.at[0], twin_rs.at[0], twin
+    )
     whole = acc[...]
     squares = jnp.sum((whole * whole).reshape(32, 8, COLS), axis=0)
     norm_box[ctx] = (
         squares[:, :128] + squares[:, 128:256] + squares[:, 256:384] + squares[:, 384:]
     )
     norm_copies = []
-    for ahead in ctx_order:
+    for ahead in ctx_order + [0]:
         place = norm_box.at[ctx]
+        if ahead:
+            norm_copies.append(
+                send(
+                    place, place, norm_ss.at[0, ahead], norm_rs.at[0, ahead],
+                    (dp, ctx_peer(ahead)),
+                )
+            )
         norm_copies.append(
-            send(place, place, norm_ss.at[ahead], norm_rs.at[ahead], (dp, ctx_peer(ahead)))
-        )
-
-    for place in range(32):
-        r, w = (place // 2) * 16, (place % 2) * FEAT
-        rs_out[place] = whole[r : r + 16, w : w + FEAT].astype(BF16)
-    chip_order = [10, 8, 2, 9, 11, 6, 14, 5, 7, 13, 15, 4, 12, 1, 3, 0]
+            send(
+                place, norm_far.at[ctx], norm_ss.at[1, ahead], norm_rs.at[1, ahead],
+                (far_dp, ctx_peer(ahead)),
+            )
+        )
+    for copy in norm_copies:
+        copy.wait_recv()
+
+    def factor_of(box):
+        total_sq = jnp.sum(jnp.sum(box[...], axis=0), axis=(0, 1), keepdims=True)
+        return scale_total / (jnp.sqrt(total_sq) + gamma_floor)
+
+    near_factor = factor_of(norm_box)
+    far_factor = factor_of(norm_far)
+    half_copy.wait_recv()
+    mixed = acc[:, aligned(core, FEAT)] * near_factor + half_in[...] * far_factor
+    rs_out[...] = mixed.astype(BF16).reshape(CHIPS, 16, FEAT)
+
+    chip_order = [10, 8, 2, 9, 11, 6, 14, 5, 7, 13, 15, 4, 12, 1, 3]
     rs_copies = []
     for step in chip_order:
-        for side in range(2):
-            if step == 0 and side == 0:
-                continue
-            other = chip_peer(step) * 2 + lax.rem(core + side, 2)
-            rs_copies.append(
-                send(
-                    rs_out.at[other], rs_in.at[dp], rs_ss.at[step * 2 + side],
-                    rs_rs.at[step * 2 + side], (other, ctx),
-                )
-            )
-    rs_in[dp] = rs_out[dp]
-    for copy in norm_copies:
+        other = chip_peer(step)
+        rs_copies.append(
+            send(
+                rs_out.at[other], rs_in.at[chip], rs_ss.at[step], rs_rs.at[step],
+                (other * 2 + core, ctx),
+            )
+        )
+    rs_in[chip] = rs_out[chip]
+    for copy in rs_copies:
         copy.wait_recv()
 
-    total_sq = jnp.sum(jnp.sum(norm_box[...], axis=0), axis=(0, 1), keepdims=True)
-    factor = scale_total / (jnp.sqrt(total_sq) + gamma_floor)
-    fac[dp] = jnp.broadcast_to(factor, (8, 128))
-    fac_copies = []
-    for step in chip_order:
-        for side in range(2):
-            if step == 0 and side == 0:
-                continue
-            other = chip_peer(step) * 2 + lax.rem(core + side, 2)
-            fac_copies.append(
-                send(
-                    fac.at[dp], fac.at[dp], fac_ss.at[step * 2 + side],
-                    fac_rs.at[step * 2 + side], (other, ctx),
-                )
-            )
-
-    for copy in rs_copies + fac_copies:
-        copy.wait_recv()
-
-    piece = jnp.zeros((16, FEAT), F32)
-    for place in range(32):
-        row = fac[place, 0:1, :]
-        piece += rs_in[place].astype(F32) * jnp.concatenate([row, row], axis=1)
+    piece = rs_in[0].astype(F32)
+    for place in range(1, CHIPS):
+        piece += rs_in[place].astype(F32)
     ag[chip] = piece.astype(BF16)
     ag_copies = []
-    for step in chip_order[:-1]:
+    for step in chip_order:
         other = chip_peer(step)
         ag_copies.append(
             send(
@@ -448,25 +446,23 @@
     for copy in ag_copies:
         copy.wait_recv()
 
-    last = send(ag, ag_far, twin_ss.at[0], twin_rs.at[0], twin)
-    for place in range(CHIPS):
-        out_ref[place * 16 : place * 16 + 16, aligned(core, FEAT)] = ag[place].astype(F32)
-    last.wait_recv()
-    for place in range(CHIPS):
-        out_ref[place * 16 : place * 16 + 16, aligned(1 - core, FEAT)] = ag_far[place].astype(F32)
+    half = out_ref.at[:, :, aligned(core, FEAT)]
+    send(ag, half, twin_ss.at[1], twin_rs.at[1], twin)
+    keep = pltpu.make_async_copy(ag, half, own_sem.at[10])
+    keep.start()
+    keep.wait()
     finish()
 
 
 def on_device(hidden_in, query_states, key_states, value_states, out_grad, span_order):
     scale_total = math.sqrt(hidden_in.shape[2] * COLS / lax.axis_size("dp"))
-    vmem = pl.BlockSpec(memory_space=pltpu.VMEM)
     dma = pltpu.SemaphoreType.DMA
-    return pl.pallas_call(
+    summed = pl.pallas_call(
         functools.partial(kernel, scale_total),
         name="clipped_grads",
-        out_shape=jax.ShapeDtypeStruct((FEAT, COLS), F32),
+        out_shape=jax.ShapeDtypeStruct((CHIPS, 16, COLS), BF16),
         in_specs=[pl.BlockSpec(memory_space=pl.ANY)] * 6,
-        out_specs=vmem,
+        out_specs=pl.BlockSpec(memory_space=pl.ANY),
         scratch_shapes=[
             pltpu.VMEM((16 * TOK, FEAT), BF16),
             pltpu.VMEM((32, SPAN, 6 * HEAD), BF16),
@@ -484,9 +480,9 @@
             pltpu.VMEM((32, SPAN, COLS), BF16),
             pltpu.VMEM((FEAT, COLS), F32),
             pltpu.VMEM((16, 8, 128), F32),
-            pltpu.VMEM((32, 8, 128), F32),
-            pltpu.VMEM((32, 16, FEAT), BF16),
-            pltpu.VMEM((32, 16, FEAT), BF16),
+            pltpu.VMEM((16, 8, 128), F32),
+            pltpu.VMEM((FEAT, FEAT), F32),
+            pltpu.VMEM((CHIPS, 16, FEAT), BF16),
             pltpu.VMEM((CHIPS, 16, FEAT), BF16),
             pltpu.VMEM((CHIPS, 16, FEAT), BF16),
             pltpu.SMEM((1, 32), jnp.int32),
@@ -495,16 +491,16 @@
             dma((6, 2, 5)), dma((6, 2, 5)),
             dma((2,)), dma((2,)),
             dma((6, 8)), dma((6, 8)),
+            dma((2, 16)), dma((2, 16)),
             dma((16,)), dma((16,)),
-            dma((32,)), dma((32,)),
-            dma((32,)), dma((32,)),
             dma((16,)), dma((16,)),
-            dma((10,)),
+            dma((11,)),
         ],
         compiler_params=pltpu.CompilerParams(
             collective_id=0, has_side_effects=True, vmem_limit_bytes=62 << 20
         ),
     )(hidden_in, query_states, key_states, value_states, out_grad, span_order)
+    return summed.astype(F32).reshape(FEAT, COLS)
 
 
 def solution(mesh):

time: 98.8 us -> 97 us (0.982)
  local copies, waits for them, and re-layouts: 1.87 us -> 0 us
  other arithmetic: 0 us -> 1.8 us
  Pallas kernels: 96.6 us -> 95 us
    unnamed x1 -> x0, local copies, waits for them, and re-layouts: 1.87 us -> none
    reshape x0 -> x1, other arithmetic: none -> 1.8 us  [on_device(): return summed.astype(F32).reshape(FEAT, COLS)]
    pallas_call x1, Pallas kernels: 96.6 us -> 95 us  [on_device(): pl.pallas_call(functools.partial(kernel, scale_total), name='clipped_grad...]
where the time goes in v4:
time: 97 us; the launch traced here: 96.8 us
  Pallas kernels  95 us (98%)
  other arithmetic  1.8 us (2%)
    pallas_call x1, Pallas kernels, on_device(): pl.pallas_call(functools.partial(kernel, scale_total), name='clipped_grad...  95 us

profile of v4, /device:TPU:1, one launch (start us, length us, event | category | flops | bytes accessed | tf_op | source)
XLA Modules:
  0.0 96.8 jit_solution(7816730741708828534)
XLA Ops:
  0.0 95.0 %clipped_grads.1 = bf16[16,16,512]{2,1,0:T(8,128)(2,1)} custom-call(bf16[1,128,4096]{2,1,0:T(8,128)(2,1)} %h_ref.1, bf16[1,128,256]{2,1,0:T(8,128)(2,1)} %q_ref.1, bf16[1,128,128]{2,1,0:T(8,128)(2,1)} %k_ref.1, bf16[1,128,128]{2,1,0:T(8,128)(2,1)} %v_ref.1, bf16[1,128,256]{2,1,0:T(8,128)(2,1)} %do_ref.1, s32[1,32]{1,0:T(1,128)} %span_ref.1), custom_call_target="tpu_custom_call" | custom-call | tf_op jit(solution)/shard_map/clipped_grads/pallas_call | solution.py:460
  95.0 1.8 %bitcast_convert_fusion = f32[256,512]{1,0:T(8,128)} fusion(bf16[16,16,512]{2,1,0:T(8,128)(2,1)} %clipped_grads.1), kind=kLoop, calls=%fused_computation | loop fusion | flops 131072 | bytes 786432 | tf_op jit(solution)/shard_map/reshape | solution.py:503

commit v5 on v4

--- a/solution.py
+++ b/solution.py
@@ -98,6 +98,7 @@
     ag_ss,
     ag_rs,
     own_sem,
+    word,
 ):
     dp = lax.axis_index("dp")
     ctx = lax.axis_index("ctx")
@@ -156,18 +157,18 @@
     for load in loads:
         load.start()
 
+    def signal(sem, *devices):
+        for device in devices:
+            pl.semaphore_signal(sem, inc=1, device_id=device, device_id_type=MESH)
+
+    x_near = [(chip_peer(step) * 2 + core, ctx) for step in (1, 3)]
+    y_near = [(chip_peer(step) * 2 + core, ctx) for step in (4, 12)]
     barrier = pltpu.get_barrier_semaphore()
-    for step in ctx_order:
-        for device in (
-            (dp, ctx_peer(step)),
-            (far_dp, ctx_peer(step)),
-            (chip_peer(step) * 2 + core, ctx),
-        ):
-            pl.semaphore_signal(barrier, inc=1, device_id=device, device_id_type=MESH)
-    pl.semaphore_signal(barrier, inc=1, device_id=twin, device_id_type=MESH)
+    signal(barrier, up, down, pair, twin, *x_near, *y_near)
     for load in loads:
         load.wait()
-    pl.semaphore_wait(barrier, 46)
+    pl.semaphore_wait(barrier, 8)
+    signal(word.at[0], *x_near)
 
     def ring_send(lane, step, view_up, view_down):
         return (
@@ -274,6 +275,9 @@
     for copy in forwards:
         copy.wait_recv()
 
+    signal(word.at[3], twin)
+    pl.semaphore_wait(word.at[0], 2)
+    signal(word.at[1], *y_near)
     send_features([9, 7, 11, 5, 13, 3, 15, 1])
 
     def place_block(block, carry):
@@ -365,6 +369,9 @@
     grads[:, :, 256:384] = (key_acc[...] * inv_scale).astype(BF16).reshape(32, SPAN, 128)
     grads[:, :, 384:] = value_acc[...].astype(BF16).reshape(32, SPAN, 128)
 
+    pl.semaphore_wait(word.at[1], 2)
+    signal(word.at[2], *y_near)
+
     own_copy.wait()
     for copy in hid_copies:
         copy.wait_recv()
@@ -387,6 +394,7 @@
     norm_box[ctx] = (
         squares[:, :128] + squares[:, 128:256] + squares[:, 256:384] + squares[:, 384:]
     )
+    pl.semaphore_wait(word.at[3], 1)
     norm_copies = []
     for ahead in ctx_order + [0]:
         place = norm_box.at[ctx]
@@ -417,6 +425,7 @@
     rs_out[...] = mixed.astype(BF16).reshape(CHIPS, 16, FEAT)
 
     chip_order = [10, 8, 2, 9, 11, 6, 14, 5, 7, 13, 15, 4, 12, 1, 3]
+    pl.semaphore_wait(word.at[2], 2)
     rs_copies = []
     for step in chip_order:
         other = chip_peer(step)
@@ -495,6 +504,7 @@
             dma((16,)), dma((16,)),
             dma((16,)), dma((16,)),
             dma((11,)),
+            pltpu.SemaphoreType.REGULAR((4,)),
         ],
         compiler_params=pltpu.CompilerParams(
             collective_id=0, has_side_effects=True, vmem_limit_bytes=62 << 20

time: 97 us -> 93.8 us (0.967)
  Pallas kernels: 95 us -> 91.8 us
    pallas_call x1, Pallas kernels: 95 us -> 91.8 us  [on_device(): pl.pallas_call(functools.partial(kernel, scale_total), name='clipped_grad...]
where the time goes in v5:
time: 93.8 us; the launch traced here: 93.6 us
  Pallas kernels  91.8 us (98%)
  other arithmetic  1.8 us (2%)
    pallas_call x1, Pallas kernels, on_device(): pl.pallas_call(functools.partial(kernel, scale_total), name='clipped_grad...  91.8 us

profile of v5, /device:TPU:1, one launch (start us, length us, event | category | flops | bytes accessed | tf_op | source)
XLA Modules:
  0.0 93.6 jit_solution(1156170242907427358)
XLA Ops:
  0.0 91.8 %clipped_grads.1 = bf16[16,16,512]{2,1,0:T(8,128)(2,1)} custom-call(bf16[1,128,4096]{2,1,0:T(8,128)(2,1)} %h_ref.1, bf16[1,128,256]{2,1,0:T(8,128)(2,1)} %q_ref.1, bf16[1,128,128]{2,1,0:T(8,128)(2,1)} %k_ref.1, bf16[1,128,128]{2,1,0:T(8,128)(2,1)} %v_ref.1, bf16[1,128,256]{2,1,0:T(8,128)(2,1)} %do_ref.1, s32[1,32]{1,0:T(1,128)} %span_ref.1), custom_call_target="tpu_custom_call" | custom-call | tf_op jit(solution)/shard_map/clipped_grads/pallas_call | solution.py:469
  91.8 1.8 %bitcast_convert_fusion = f32[256,512]{1,0:T(8,128)} fusion(bf16[16,16,512]{2,1,0:T(8,128)(2,1)} %clipped_grads.1), kind=kLoop, calls=%fused_computation | loop fusion | flops 131072 | bytes 786432 | tf_op jit(solution)/shard_map/reshape | solution.py:513

commit v6 on v5

--- a/solution.py
+++ b/solution.py
@@ -267,7 +267,7 @@
                 )
             )
 
-    early = {3: [8], 4: [6, 10, 4, 12, 2, 14]}
+    early = {}
     for step in range(1, 5):
         for lane in lanes:
             next(lane)
@@ -278,7 +278,7 @@
     signal(word.at[3], twin)
     pl.semaphore_wait(word.at[0], 2)
     signal(word.at[1], *y_near)
-    send_features([9, 7, 11, 5, 13, 3, 15, 1])
+    send_features([8, 9, 7, 10, 6, 11, 5, 12, 4, 13, 3, 14, 2, 15, 1])
 
     def place_block(block, carry):
         rows = raw[slots[block]]
@@ -372,19 +372,31 @@
     pl.semaphore_wait(word.at[1], 2)
     signal(word.at[2], *y_near)
 
+    def wait_features(ahead):
+        source = h_ref.at[0, :, mine_features]
+        pltpu.make_async_remote_copy(
+            src_ref=source, dst_ref=hid.at[mine, :],
+            send_sem=hid_ss.at[ahead], recv_sem=hid_rs.at[ahead],
+            device_id=pair, device_id_type=MESH,
+        ).wait_recv()
+
+    mine_features = aligned(ctx, FEAT)
     own_copy.wait()
-    for copy in hid_copies:
-        copy.wait_recv()
-
-    for block in range(NZ):
-        part = jnp.concatenate(
-            [grads[spans[0, block * 4 + s]] for s in range(4)], axis=0
-        )
-        part = contract(hid[block * 256 : (block + 1) * 256, :], part, 0, 0)
-        if block == 0:
+    for n, shift in enumerate([4, 3, 5, 2, 6, 1, 7, 0]):
+        if shift:
+            for ahead in (2 * shift + yl, 2 * shift + yl - 1):
+                wait_features(ahead)
+        else:
+            wait_features(15 - 14 * yl)
+        block = zed(-shift)
+        part = jnp.concatenate([grads[spans[0, block * 4 + s]] for s in range(4)], axis=0)
+        part = contract(hid[aligned(block, 256), :], part, 0, 0)
+        if n == 0:
             acc[...] = part
         else:
             acc[...] += part
+    for copy in hid_copies:
+        copy.open_recv = False
 
     half_copy = send(
         acc.at[:, aligned(1 - core, FEAT)], half_in, twin_ss.at[0], twin_rs.at[0], twin

time: 93.8 us -> 93.7 us (level)
  no operation moved by 1% of the time
where the time goes in v6:
time: 93.7 us; the launch traced here: 93.4 us
  Pallas kernels  91.6 us (98%)
  other arithmetic  1.8 us (2%)
    pallas_call x1, Pallas kernels, on_device(): pl.pallas_call(functools.partial(kernel, scale_total), name='clipped_grad...  91.6 us

profile of v6, /device:TPU:1, one launch (start us, length us, event | category | flops | bytes accessed | tf_op | source)
XLA Modules:
  0.0 93.4 jit_solution(13409017532446269311)
XLA Ops:
  0.0 91.6 %clipped_grads.1 = bf16[16,16,512]{2,1,0:T(8,128)(2,1)} custom-call(bf16[1,128,4096]{2,1,0:T(8,128)(2,1)} %h_ref.1, bf16[1,128,256]{2,1,0:T(8,128)(2,1)} %q_ref.1, bf16[1,128,128]{2,1,0:T(8,128)(2,1)} %k_ref.1, bf16[1,128,128]{2,1,0:T(8,128)(2,1)} %v_ref.1, bf16[1,128,256]{2,1,0:T(8,128)(2,1)} %do_ref.1, s32[1,32]{1,0:T(1,128)} %span_ref.1), custom_call_target="tpu_custom_call" | custom-call | tf_op jit(solution)/shard_map/clipped_grads/pallas_call | solution.py:481
  91.6 1.8 %bitcast_convert_fusion = f32[256,512]{1,0:T(8,128)} fusion(bf16[16,16,512]{2,1,0:T(8,128)(2,1)} %clipped_grads.1), kind=kLoop, calls=%fused_computation | loop fusion | flops 131072 | bytes 786432 | tf_op jit(solution)/shard_map/reshape | solution.py:525

commit v7 on v6

--- a/solution.py
+++ b/solution.py
@@ -267,7 +267,7 @@
                 )
             )
 
-    early = {}
+    early = {4: [8, 6, 10]}
     for step in range(1, 5):
         for lane in lanes:
             next(lane)
@@ -278,7 +278,7 @@
     signal(word.at[3], twin)
     pl.semaphore_wait(word.at[0], 2)
     signal(word.at[1], *y_near)
-    send_features([8, 9, 7, 10, 6, 11, 5, 12, 4, 13, 3, 14, 2, 15, 1])
+    send_features([9, 7, 11, 5, 12, 4, 13, 3, 14, 2, 15, 1])
 
     def place_block(block, carry):
         rows = raw[slots[block]]

time: 93.7 us -> 91.2 us (0.973)
  Pallas kernels: 91.6 us -> 89.1 us
    pallas_call x1, Pallas kernels: 91.6 us -> 89.1 us  [on_device(): pl.pallas_call(functools.partial(kernel, scale_total), name='clipped_grad...]
where the time goes in v7:
time: 91.2 us; the launch traced here: 91 us
  Pallas kernels  89.1 us (98%)
  other arithmetic  1.8 us (2%)
    pallas_call x1, Pallas kernels, on_device(): pl.pallas_call(functools.partial(kernel, scale_total), name='clipped_grad...  89.1 us

profile of v7, /device:TPU:1, one launch (start us, length us, event | category | flops | bytes accessed | tf_op | source)
XLA Modules:
  0.0 91.0 jit_solution(2570984945207887437)
XLA Ops:
  0.0 89.1 %clipped_grads.1 = bf16[16,16,512]{2,1,0:T(8,128)(2,1)} custom-call(bf16[1,128,4096]{2,1,0:T(8,128)(2,1)} %h_ref.1, bf16[1,128,256]{2,1,0:T(8,128)(2,1)} %q_ref.1, bf16[1,128,128]{2,1,0:T(8,128)(2,1)} %k_ref.1, bf16[1,128,128]{2,1,0:T(8,128)(2,1)} %v_ref.1, bf16[1,128,256]{2,1,0:T(8,128)(2,1)} %do_ref.1, s32[1,32]{1,0:T(1,128)} %span_ref.1), custom_call_target="tpu_custom_call" | custom-call | tf_op jit(solution)/shard_map/clipped_grads/pallas_call | solution.py:481
  89.1 1.8 %bitcast_convert_fusion = f32[256,512]{1,0:T(8,128)} fusion(bf16[16,16,512]{2,1,0:T(8,128)(2,1)} %clipped_grads.1), kind=kLoop, calls=%fused_computation | loop fusion | flops 131072 | bytes 786432 | tf_op jit(solution)/shard_map/reshape | solution.py:525
